TPU v7x, 32 devices: a whole 2x2x4 slice. The times are simulated.
32 devices in a mesh: sec: 16 (over z, y, x), mpo: 2 (over core).
Axes of the slice: x: 2, y: 2, z: 4, core: 2. Of those that a mesh axis runs over, the one named last changes fastest.
Arguments:
- wavefunction: bfloat16 [16, 8, 512, 256], P('sec', None, 'mpo'), may hold values from -6 to 6
- left_env: bfloat16 [16, 40, 512, 512], P('sec', 'mpo'), may hold values from -0.0390625 to 0.0390625
- right_env: bfloat16 [16, 40, 256, 256], P('sec', 'mpo'), may hold values from -0.375 to 0.375
- left_dims: int32 [16], P('sec'), may hold values from 256 to 512
- right_dims: int32 [16], P('sec'), may hold values from 128 to 256
- term_shift: int32 [40], P('mpo'), may hold values from 0 to 4, as said below
Outputs:
- product: bfloat16 [16, 8, 512, 256], P('sec', None, 'mpo')
Inputs may be any that keep to these rules, and one draw needn't show every extreme that they name: `term_shift`: each of the five classes is named by exactly 8 terms.
All inputs are finite; a program needn't handle non-finite values.
Results may differ from a plain program's by a relative error of at most 0.0049.
Values may be sent and summed in bfloat16 or wider, within the bound.
No kernel may reach another device: no remote copies, remote signals or barrier semaphores. Data moves between devices by JAX's collectives and lax.ppermute only.
A program may use at most 192 MiB of HBM per device.

v0:
```python
import jax
import jax.numpy as jnp
from jax import lax
from jax.sharding import PartitionSpec as P

SPINS = 8


number_steps = (0, 1, -1, 1, -1)
spin_steps = (0, 1, -1, -1, 1)


def shifted(array, axis, by):
    length = lax.axis_size(axis)
    pairs = [(i, i + by) for i in range(length) if 0 <= i + by < length]
    return lax.ppermute(array, axis, pairs)


def per_device(wavefunction, left_env, right_env, left_dims, right_dims, term_shift):
    row_share = wavefunction.shape[2]
    columns = wavefunction.shape[3]
    mpo_place = lax.axis_index("mpo")
    sector_id = lax.axis_index("sec")
    lattice_rows = lax.axis_size("sec") // SPINS
    rows_here = mpo_place * row_share + jnp.arange(row_share, dtype=jnp.int32)
    column_ids = jnp.arange(columns, dtype=jnp.int32)
    keep_mask = (rows_here[:, None] < left_dims[0]) & (column_ids[None, :] < right_dims[0])
    live_block = jnp.where(keep_mask[None, None], wavefunction, jnp.zeros_like(wavefunction))
    sector_line = sector_id // SPINS
    sector_place = sector_id % SPINS
    line_steps = jnp.array(number_steps, dtype=jnp.int32)
    place_steps = jnp.array(spin_steps, dtype=jnp.int32)
    source_line = sector_line - line_steps
    source_place = sector_place - place_steps
    inside = (
        (source_line >= 0)
        & (source_line < lattice_rows)
        & (source_place >= 0)
        & (source_place < SPINS)
    )
    selector = (
        (term_shift[:, None] == jnp.arange(5, dtype=jnp.int32)[None, :]) & inside[None, :]
    ).astype(jnp.bfloat16)
    neighbours = [live_block]
    for shift_class in range(1, 5):
        offset = number_steps[shift_class] * SPINS + spin_steps[shift_class]
        neighbours.append(shifted(live_block, "sec", offset))
    stacked = lax.all_gather(jnp.concatenate(neighbours, axis=0), "mpo", axis=2, tiled=True)
    selected = jnp.einsum(
        "tc,cvpq->tvpq", selector, stacked, preferred_element_type=jnp.float32
    ).astype(jnp.bfloat16)
    left_terms = left_env[0]
    right_terms = right_env[0]
    applied = jnp.einsum(
        "tpk,tvkq->tvpq", left_terms, selected, preferred_element_type=jnp.float32
    ).astype(jnp.bfloat16)
    term_total = jnp.einsum(
        "tvpk,tqk->vpq", applied, right_terms, preferred_element_type=jnp.float32
    )[None]
    row_sums = lax.psum_scatter(term_total, "mpo", scatter_dimension=2, tiled=True)
    return jnp.where(keep_mask[None, None], row_sums, jnp.zeros_like(row_sums)).astype(jnp.bfloat16)


def solution(mesh):
    in_specs = (
        P("sec", None, "mpo", None),
        P("sec", "mpo", None, None),
        P("sec", "mpo", None, None),
        P("sec"),
        P("sec"),
        P("mpo"),
    )
    out_specs = P("sec", None, "mpo", None)
    return jax.shard_map(
        per_device, mesh=mesh, in_specs=in_specs, out_specs=out_specs, check_vma=False
    )
```

profile of v0, /device:TPU:25, one launch (start us, length us, event | category | flops | bytes accessed | tf_op | source)
XLA Modules:
  0.0 249.0 jit_solution(9697755988486384912)
XLA Ops:
  6.5 0.0 copy-start
  6.5 0.0 copy-start.1
  6.5 0.0 copy-start.2
  6.5 0.0 copy-start.3
  6.5 0.0 all-gather.2.cloned.1.call-start
  8.1 0.1 broadcast_and_fusion
  8.2 2.4 constant_dynamic-update-slice_fusion.4
  10.6 1.3 collective-permute-start
  11.9 7.7 %collective-permute-start.1 = (bf16[1,8,256,256]{3,2,1,0:T(8,128)(2,1)S(1)}, bf16[1,8,256,256]{3,2,1,0:T(8,128)(2,1)S(1)}, u32[]{:S(2)}, u32[]{:S(2)}) collective-permute-start(bf16[1,8,256,256]{3,2,1,0:T(8,128)(2,1)S(1)} %get-tuple-element.6), channel_id=1, source_target_pairs={{18,0},{20,2},{22,4},{24,6},{26,8},{28,10},{30,12},{19,1},{21,3},{... | collective-permute-start | bytes 3145736 | tf_op jit(solution)/shard_map/ppermute | solution.py:16
  19.6 1.3 collective-permute-start.2
  20.9 5.9 %collective-permute-start.3 = (bf16[1,8,256,256]{3,2,1,0:T(8,128)(2,1)S(1)}, bf16[1,8,256,256]{3,2,1,0:T(8,128)(2,1)S(1)}, u32[]{:S(2)}, u32[]{:S(2)}) collective-permute-start(bf16[1,8,256,256]{3,2,1,0:T(8,128)(2,1)S(1)} %get-tuple-element.6), channel_id=1, source_target_pairs={{14,0},{16,2},{18,4},{20,6},{22,8},{24,10},{26,12},{28,14},{30,16}... | collective-permute-start | bytes 3145736 | tf_op jit(solution)/shard_map/ppermute | solution.py:16
  26.8 13.3 %collective-permute-done = bf16[1,8,256,256]{3,2,1,0:T(8,128)(2,1)S(1)} collective-permute-done((bf16[1,8,256,256]{3,2,1,0:T(8,128)(2,1)S(1)}, bf16[1,8,256,256]{3,2,1,0:T(8,128)(2,1)S(1)}, u32[]{:S(2)}, u32[]{:S(2)}) %collective-permute-start) | collective-permute-done | bytes 1048608 | tf_op jit(solution)/shard_map/ppermute | solution.py:16
  40.1 1.1 constant_dynamic-update-slice_fusion.3
  41.2 0.0 collective-permute-done.1
  41.2 1.0 constant_dynamic-update-slice_fusion.2
  42.3 65.3 %collective-permute-done.2 = bf16[1,8,256,256]{3,2,1,0:T(8,128)(2,1)S(1)} collective-permute-done((bf16[1,8,256,256]{3,2,1,0:T(8,128)(2,1)S(1)}, bf16[1,8,256,256]{3,2,1,0:T(8,128)(2,1)S(1)}, u32[]{:S(2)}, u32[]{:S(2)}) %collective-permute-start.2) | collective-permute-done | bytes 1048608 | tf_op jit(solution)/shard_map/ppermute | solution.py:16
  107.6 1.1 constant_dynamic-update-slice_fusion.1
  108.7 0.0 collective-permute-done.3
  108.7 1.0 constant_dynamic-update-slice_fusion
  109.7 0.0 all-gather.2.cloned.1.call-update
  109.7 0.0 reduce-scatter.2.cloned.1.call-start
  109.8 0.0 copy-done.1
  109.8 0.0 copy-done.2
  109.8 24.6 %all-gather.2.cloned.1.call-done = bf16[5,8,512,256]{3,2,1,0:T(8,128)(2,1)} async-done(((bf16[5,8,256,256]{3,2,1,0:T(8,128)(2,1)}), bf16[5,8,512,256]{3,2,1,0:T(8,128)(2,1)}) %all-gather.2.cloned.1.call-update) | async-done | bytes 10485776 | tf_op jit(solution)/shard_map/all_gather | solution.py:48
  134.5 0.0 copy-done.3
  134.5 29.9 %fusion.9 = bf16[20,8,512,256]{3,0,2,1:T(8,128)(2,1)} fusion(bf16[5,8,512,256]{3,2,1,0:T(8,128)(2,1)} %all-gather.2.cloned.1.call-done, s32[20]{0:T(128)S(1)} %copy-done.3, pred[5]{0:T(512)(128)(4,1)S(1)} %compare_and_fusion), kind=kOutput, calls=%fused_computation.6 | convolution fusion | flops 209715392 | bytes 52428884 | tf_op jit(solution)/shard_map/tc,cvpq->tvpq/dot_general | solution.py:49
  164.4 42.5 %fusion.44 = bf16[20,8,512,256]{3,2,0,1:T(8,128)(2,1)} fusion(bf16[1,20,512,512]{3,2,1,0:T(8,128)(2,1)} %param.9, bf16[20,8,512,256]{3,0,2,1:T(8,128)(2,1)} %fusion.9), kind=kOutput, calls=%fused_computation.2.clone.clone.clone.1 | convolution fusion | flops 21495808000 | bytes 94371840 | tf_op jit(solution)/shard_map/tpk,tvkq->tvpq/dot_general | solution.py:54
  206.9 0.0 copy-done
  206.9 19.1 %fusion.14 = f32[1,8,512,256]{3,2,1,0:T(8,128)} fusion(bf16[1,20,256,256]{3,2,1,0:T(8,128)(2,1)S(1)} %copy-done, bf16[20,8,512,256]{3,2,0,1:T(8,128)(2,1)} %fusion.44), kind=kOutput, calls=%fused_computation.10 | convolution fusion | flops 10737418240 | bytes 48758784 | tf_op jit(solution)/shard_map/tvpk,tqk->vpq/dot_general | solution.py:57
  226.0 0.0 reduce-scatter.2.cloned.1.call-update
  226.0 13.4 %reduce-scatter.2.cloned.1.call-done = f32[1,8,256,256]{3,2,1,0:T(8,128)} async-done(((f32[1,8,512,256]{3,2,1,0:T(8,128)}), f32[1,8,256,256]{3,2,1,0:T(8,128)}) %reduce-scatter.2.cloned.1.call-update) | async-done | bytes 2097168 | tf_op jit(solution)/shard_map/reduce_scatter | solution.py:60
  239.4 2.8 %select_convert_fusion = bf16[1,8,256,256]{3,2,1,0:T(8,128)(2,1)} fusion(f32[1,8,256,256]{3,2,1,0:T(8,128)} %reduce-scatter.2.cloned.1.call-done, pred[256,256]{1,0:T(8,128)(4,1)S(1)} %broadcast_and_fusion), kind=kLoop, calls=%fused_computation.11 | loop fusion | flops 524288 | bytes 3211264 | tf_op jit(solution)/shard_map/convert_element_type | solution.py:61
  (2 shorter events, 0.0 us)
Async XLA Ops:
  6.5 200.3 %copy-start = (bf16[1,20,256,256]{3,2,1,0:T(8,128)(2,1)S(1)}, bf16[1,20,256,256]{3,2,1,0:T(8,128)(2,1)}, u32[]{:S(2)}) copy-start(bf16[1,20,256,256]{3,2,1,0:T(8,128)(2,1)} %param.10) | copy-start | bytes 7864324
  6.5 103.3 %copy-start.1 = (s32[5]{0:T(128)S(1)}, s32[5]{0:T(128)}, u32[]{:S(2)}) copy-start(s32[5]{0:T(128)} %constant.56) | copy-start | bytes 64
  6.5 103.3 %copy-start.2 = (s32[5]{0:T(128)S(1)}, s32[5]{0:T(128)}, u32[]{:S(2)}) copy-start(s32[5]{0:T(128)} %constant.55) | copy-start | bytes 64
  6.5 128.0 %copy-start.3 = (s32[20]{0:T(128)S(1)}, s32[20]{0:T(128)}, u32[]{:S(2)}) copy-start(s32[20]{0:T(128)} %param.13) | copy-start | bytes 244
  6.5 127.9 %all-gather.2.cloned.1.call-start = ((), (), s32[]{:S(2)}) async-start(), calls=%async_computation.1 | async-start | bytes 15728640 | tf_op jit(solution)/shard_map/all_gather | solution.py:48
  10.6 29.5 %collective-permute-start = (bf16[1,8,256,256]{3,2,1,0:T(8,128)(2,1)S(1)}, bf16[1,8,256,256]{3,2,1,0:T(8,128)(2,1)S(1)}, u32[]{:S(2)}, u32[]{:S(2)}) collective-permute-start(bf16[1,8,256,256]{3,2,1,0:T(8,128)(2,1)S(1)} %get-tuple-element.6), channel_id=1, source_target_pairs={{0,18},{2,20},{4,22},{6,24},{8,26},{10,28},{12,30},{1,19},{3,21},{... | collective-permute-start | bytes 3145736 | tf_op jit(solution)/shard_map/ppermute | solution.py:16
  11.9 29.3 %collective-permute-start.1 = (bf16[1,8,256,256]{3,2,1,0:T(8,128)(2,1)S(1)}, bf16[1,8,256,256]{3,2,1,0:T(8,128)(2,1)S(1)}, u32[]{:S(2)}, u32[]{:S(2)}) collective-permute-start(bf16[1,8,256,256]{3,2,1,0:T(8,128)(2,1)S(1)} %get-tuple-element.6), channel_id=1, source_target_pairs={{18,0},{20,2},{22,4},{24,6},{26,8},{28,10},{30,12},{19,1},{21,3},{... | collective-permute-start | bytes 3145736 | tf_op jit(solution)/shard_map/ppermute | solution.py:16
  19.6 88.0 %collective-permute-start.2 = (bf16[1,8,256,256]{3,2,1,0:T(8,128)(2,1)S(1)}, bf16[1,8,256,256]{3,2,1,0:T(8,128)(2,1)S(1)}, u32[]{:S(2)}, u32[]{:S(2)}) collective-permute-start(bf16[1,8,256,256]{3,2,1,0:T(8,128)(2,1)S(1)} %get-tuple-element.6), channel_id=1, source_target_pairs={{0,14},{2,16},{4,18},{6,20},{8,22},{10,24},{12,26},{14,28},{16,30}... | collective-permute-start | bytes 3145736 | tf_op jit(solution)/shard_map/ppermute | solution.py:16
  20.9 87.8 %collective-permute-start.3 = (bf16[1,8,256,256]{3,2,1,0:T(8,128)(2,1)S(1)}, bf16[1,8,256,256]{3,2,1,0:T(8,128)(2,1)S(1)}, u32[]{:S(2)}, u32[]{:S(2)}) collective-permute-start(bf16[1,8,256,256]{3,2,1,0:T(8,128)(2,1)S(1)} %get-tuple-element.6), channel_id=1, source_target_pairs={{14,0},{16,2},{18,4},{20,6},{22,8},{24,10},{26,12},{28,14},{30,16}... | collective-permute-start | bytes 3145736 | tf_op jit(solution)/shard_map/ppermute | solution.py:16
  109.7 129.6 %reduce-scatter.2.cloned.1.call-start = ((), (), s32[]{:S(2)}) async-start(), calls=%async_computation.2 | async-start | bytes 6291456 | tf_op jit(solution)/shard_map/reduce_scatter | solution.py:60
Sparse Core Ops, SparseCore 0:
  109.9 24.5 all-gather.1
  226.1 13.2 reduce-scatter.1
where the time goes:
time: 250 us; the launch traced here: 249 us
  waiting for transfers between devices  117 us (47%)
  matrix products  91.5 us (37%)
  starting transfers between devices  16.3 us (7%)
  between operations  15 us (6%)
  other arithmetic  5.29 us (2%)
  local copies, waits for them, and re-layouts  4.23 us (2%)
    ppermute x4, waiting for transfers between devices, shifted(): return lax.ppermute(array, axis, pairs)  78.7 us
    dot_general x1, matrix products, per_device(): jnp.einsum('tpk,tvkq->tvpq', left_terms, selected, preferred_element_type...  42.5 us
    dot_general x1, matrix products, per_device(): jnp.einsum('tc,cvpq->tvpq', selector, stacked, preferred_element_type=jnp...  29.9 us
    all_gather x1, waiting for transfers between devices, per_device(): lax.all_gather(jnp.concatenate(neighbours, axis=0), 'mpo', axis=2, tiled=...  24.6 us
    dot_general x1, matrix products, per_device(): jnp.einsum('tvpk,tqk->vpq', applied, right_terms, preferred_element_type=...  19.1 us
    ppermute x4, starting transfers between devices, shifted(): return lax.ppermute(array, axis, pairs)  16.2 us
    reduce_scatter x1, waiting for transfers between devices, per_device(): lax.psum_scatter(term_total, 'mpo', scatter_dimension=2, tiled=True)  13.4 us
  transfers between devices with their start and end apart: 6, of which 4 were waited for; matrix products, arithmetic and copies ran while one was open for 1% of the time, Pallas kernels for 0%

commit v1 on v0

v1 whole, which is shorter than its diff:
```python
import functools

import jax
import jax.numpy as jnp
from jax import lax
from jax.experimental import pallas as pl
from jax.experimental.pallas import tpu as pltpu
from jax.sharding import PartitionSpec as P

SPINS = 8
CLASSES = 5


def sum_terms(slots, ways, resume, finish, mask, group, shift_ref, meta_ref, *refs):
    parts, refs = refs[:ways], refs[ways:]
    left_ref, right_ref, refs = refs[0], refs[1], refs[2:]
    if resume is not None:
        before_ref, refs = refs[0], refs[1:]
    if finish:
        keep_ref, give_refs, refs = refs[0], refs[1:ways], refs[ways:]
    else:
        total, refs = refs[0], refs[1:]
    left_buf, right_buf, source, applied, refs = refs[0], refs[1], refs[2], refs[3], refs[4:]
    if finish:
        total, refs = refs[0], refs[1:]
    left_sem, right_sem, part_sem, before_sem = refs
    place, shift_class = meta_ref[0], meta_ref[1]
    vectors, share, columns = parts[0].shape
    rows = share * ways

    def copy_part(turn):
        begin = pl.multiple_of(lax.rem(place + ways - turn, ways) * share, share)
        return pltpu.make_async_copy(parts[turn], source.at[:, pl.ds(begin, share), :], part_sem.at[turn])

    def copies(term, slot):
        return (
            pltpu.make_async_copy(left_ref.at[0, term], left_buf.at[slot], left_sem.at[slot]),
            pltpu.make_async_copy(right_ref.at[0, term], right_buf.at[slot], right_sem.at[slot]),
        )

    for turn in range(ways):
        copy_part(turn).start()

    def fetch(term, count):
        hit = (shift_ref[term] == shift_class) & (count < slots)

        @pl.when(hit)
        def _():
            for copy in copies(term, count):
                copy.start()

        return count + hit.astype(jnp.int32)

    count = lax.fori_loop(0, shift_ref.shape[0], fetch, jnp.int32(0))
    if resume is not None:
        copy_before = pltpu.make_async_copy(before_ref.at[pl.ds(resume, vectors)], total, before_sem)
        copy_before.start()
        copy_before.wait()
    else:
        total[...] = jnp.zeros_like(total)
    for turn in range(ways):
        copy_part(turn).wait()

    if mask:
        kept = (lax.broadcasted_iota(jnp.int32, source.shape[1:], 0) < meta_ref[2]) & (lax.broadcasted_iota(jnp.int32, source.shape[1:], 1) < meta_ref[3])
        for vector in range(vectors):
            source[vector] = jnp.where(kept, source[vector], jnp.zeros_like(source[vector]))

    def arrive(slot):
        for copy in copies(0, slot):
            copy.wait()

    def add_terms(first, group):
        rights = jnp.concatenate([right_buf[first + i] for i in range(group)], axis=1)
        for vector in range(vectors):
            for i in range(group):
                applied[vector, :, i * columns : (i + 1) * columns] = jnp.dot(
                    left_buf[first + i], source[vector], preferred_element_type=jnp.float32
                ).astype(jnp.bfloat16)
        width = group * columns
        total[...] += lax.dot_general(
            applied[:, :, :width].reshape(vectors * rows, width),
            rights,
            (((1,), (1,)), ((), ())),
            preferred_element_type=jnp.float32,
        ).reshape(total.shape)

    whole = count // group

    @pl.loop(0, whole)
    def _(turn):
        for i in range(group):
            arrive(turn * group + i)
        add_terms(turn * group, group)

    if group > 1:

        @pl.loop(whole * group, count)
        def _(slot):
            arrive(slot)
            add_terms(slot, 1)

    if finish:
        for turn in range(ways):
            begin = pl.multiple_of(lax.rem(place + turn, ways) * share, share)
            block = total[:, pl.ds(begin, share), :]
            if turn == 0:
                keep_ref[...] = block
            else:
                give_refs[turn - 1][...] = block.astype(jnp.bfloat16)


def call_terms(shift, meta, parts, left, right, before=None, start=0, finish=False, mask=False):
    ways = len(parts)
    vectors, share, columns = parts[0].shape
    rows = share * ways
    terms = left.shape[1]
    slots = min(terms, terms * ways // CLASSES)
    group = 1 if vectors >= 4 else 2
    any_spec = pl.BlockSpec(memory_space=pl.ANY)
    smem = pl.BlockSpec(memory_space=pltpu.SMEM)
    vmem = pl.BlockSpec(memory_space=pltpu.VMEM)
    operands = [shift, meta, *parts, left, right]
    in_specs = [smem, smem] + [any_spec] * (ways + 2)
    if before is not None:
        operands.append(before)
        in_specs.append(any_spec)
    whole = jax.ShapeDtypeStruct((vectors, rows, columns), jnp.float32)
    scratch = [
        pltpu.VMEM((slots, rows, rows), jnp.bfloat16),
        pltpu.VMEM((slots, columns, columns), jnp.bfloat16),
        pltpu.VMEM((vectors, rows, columns), jnp.bfloat16),
        pltpu.VMEM((vectors, rows, group * columns), jnp.bfloat16),
    ]
    if finish:
        out_shape = [jax.ShapeDtypeStruct((vectors, share, columns), jnp.float32)] + [
            jax.ShapeDtypeStruct((vectors, share, columns), jnp.bfloat16)
        ] * (ways - 1)
        out_specs = [vmem] * ways
        scratch.append(pltpu.VMEM(whole.shape, whole.dtype))
    else:
        out_shape, out_specs = whole, vmem
    scratch += [
        pltpu.SemaphoreType.DMA((slots,)),
        pltpu.SemaphoreType.DMA((slots,)),
        pltpu.SemaphoreType.DMA((ways,)),
        pltpu.SemaphoreType.DMA,
    ]
    typical = max(1, slots // ways)
    return pl.pallas_call(
        functools.partial(sum_terms, slots, ways, None if before is None else start, finish, mask, group),
        out_shape=out_shape,
        in_specs=in_specs,
        out_specs=out_specs,
        scratch_shapes=scratch,
        compiler_params=pltpu.CompilerParams(vmem_limit_bytes=40 * 2**20),
        cost_estimate=pl.CostEstimate(
            flops=typical * vectors * 2 * rows * columns * (rows + columns),
            bytes_accessed=typical * 2 * (rows * rows + columns * columns),
            transcendentals=0,
        ),
    )(*operands)


def permute(array, axis, pairs):
    return lax.ppermute(array, axis, sorted(pairs)) if pairs else jnp.zeros_like(array)


def around(array):
    ways = lax.axis_size("mpo")
    return [array] + [
        permute(array, "mpo", [(i, (i + turn) % ways) for i in range(ways)]) for turn in range(1, ways)
    ]


def per_device(wavefunction, left_env, right_env, left_dims, right_dims, term_shift):
    vectors, share, columns = wavefunction.shape[1:]
    place = lax.axis_index("mpo")
    ways = lax.axis_size("mpo")
    sector = lax.axis_index("sec")
    lines = lax.axis_size("sec") // SPINS
    line, spin = sector // SPINS, sector % SPINS
    odd = spin % 2 == 1
    row_ids = place * share + jnp.arange(share, dtype=jnp.int32)
    column_ids = jnp.arange(columns, dtype=jnp.int32)
    keep_mask = ((row_ids[:, None] < left_dims[0]) & (column_ids[None, :] < right_dims[0]))[None]

    def cross(step):
        return [
            (n * SPINS + p, (n + step) * SPINS + (p ^ 1))
            for n in range(lines)
            for p in range(SPINS)
            if 0 <= n + step < lines
        ]

    relay = [
        (n * SPINS + p, n * SPINS + p + (-2 if p % 2 else 2))
        for n in range(lines)
        for p in range(SPINS)
        if 0 <= p + (-2 if p % 2 else 2) < SPINS
    ]
    relay_here = jnp.where(odd, spin + 2 < SPINS, spin >= 2)
    from_below = (jnp.where(odd, 1, 3), jnp.where(odd, 3, 1), line > 0)
    from_above = (jnp.where(odd, 4, 2), jnp.where(odd, 2, 4), line + 1 < lines)
    if lines == 2:
        ways_across = [(cross(1) + cross(-1), tuple(jnp.where(line == 1, b, a) for b, a in zip(from_below, from_above)))]
    else:
        ways_across = [(cross(1), from_below), (cross(-1), from_above)] if lines > 1 else []

    def meta(shift_class, valid=True):
        return jnp.stack([place, jnp.where(valid, shift_class, -1), left_dims[0], right_dims[0]]).astype(jnp.int32)

    def after(array, *others):
        return lax.optimization_barrier((array, *others))[0]

    terms = functools.partial(call_terms, term_shift)
    widths = [vectors // 4] * 4 if vectors % 4 == 0 else [vectors]
    starts = [sum(widths[:i]) for i in range(len(widths))]
    count = len(widths)
    landed, near_parts, far_parts = {}, {}, {}
    last = None

    def send(index, *behind):
        block = wavefunction[0, starts[index] : starts[index] + widths[index]]
        if behind:
            block = after(block, *behind)
        block = jnp.where(keep_mask, block, jnp.zeros_like(block))
        landed[index] = [permute(block, "sec", pairs) for pairs, _ in ways_across]

    for index in range(min(2, count)):
        send(index)
    own = terms(meta(jnp.int32(0)), around(wavefunction[0]), left_env, right_env, mask=True)
    product = jnp.zeros_like(wavefunction[0])
    totals = {}

    def arrive(index, behind):
        here = [after(block, behind) for block in landed[index]]
        if index + 2 < count:
            send(index + 2, *here)
        near_parts[index] = [around(block) for block in here]
        far_parts[index] = [around(permute(block, "sec", relay)) for block in here]

    def near_terms(index):
        total, offset = own, starts[index]
        for parts, (_, (near, _, valid)) in zip(near_parts[index], ways_across):
            total = terms(meta(near, valid), parts, left_env, right_env, total, offset)
            offset = 0
        totals[index] = (total, offset)
        return total

    def far_terms(index, behind):
        total, offset = totals[index]
        for number, (parts, (_, (_, far, valid))) in enumerate(zip(far_parts[index], ways_across)):
            parts = [after(part, behind) for part in parts]
            total = terms(
                meta(far, valid & relay_here), parts, left_env, right_env, total, offset,
                number == len(ways_across) - 1,
            )
            offset = 0
        return total

    def close(index, sums, product):
        total = sums[0]
        for turn, given in enumerate(sums[1:], 1):
            total += permute(given, "mpo", [(i, (i + turn) % ways) for i in range(ways)]).astype(jnp.float32)
        block = jnp.where(keep_mask, total, jnp.zeros_like(total)).astype(jnp.bfloat16)
        return lax.dynamic_update_slice(product, block, (starts[index], 0, 0))

    before = own
    for index in range(count):
        arrive(index, before)
        before = near_terms(index)
        if index:
            sums = far_terms(index - 1, before)
            before = sums[0]
            product = close(index - 1, sums, product)
    product = close(count - 1, far_terms(count - 1, before), product)
    return product[None]


def solution(mesh):
    in_specs = (
        P("sec", None, "mpo", None),
        P("sec", "mpo", None, None),
        P("sec", "mpo", None, None),
        P("sec"),
        P("sec"),
        P("mpo"),
    )
    out_specs = P("sec", None, "mpo", None)
    return jax.shard_map(
        per_device, mesh=mesh, in_specs=in_specs, out_specs=out_specs, check_vma=False
    )
```

time: 250 us -> 101 us (0.40)
  matrix products: 91.5 us -> 0 us
  waiting for transfers between devices: 117 us -> 27.5 us
  Pallas kernels: 0 us -> 42.9 us
  between operations: 15 us -> 1.58 us
  starting transfers between devices: 16.3 us -> 20.9 us
  other arithmetic: 5.29 us -> 2.58 us
    dot_general x3 -> x0, matrix products: 91.5 us -> none  [the longest x1 42.5 us: per_device(): jnp.einsum('tpk,tvkq->tvpq', left_terms, selected, preferred_element_type...]
    ppermute x4 -> x21, waiting for transfers between devices: 78.7 us -> 27.5 us  [permute(): lax.ppermute(array, axis, sorted(pairs))]
    pallas_call x0 -> x9, Pallas kernels: none -> 42.9 us  [call_terms(): pl.pallas_call(functools.partial(sum_terms, slots, ways, None if before i...]
    all_gather x1 -> x0, waiting for transfers between devices: 24.6 us -> none  [per_device(): lax.all_gather(jnp.concatenate(neighbours, axis=0), 'mpo', axis=2, tiled=...]
    reduce_scatter x1 -> x0, waiting for transfers between devices: 13.4 us -> none  [per_device(): lax.psum_scatter(term_total, 'mpo', scatter_dimension=2, tiled=True)]
    ppermute x4 -> x21, starting transfers between devices: 16.2 us -> 20.9 us  [permute(): lax.ppermute(array, axis, sorted(pairs))]
    convert_element_type x1, other arithmetic: 2.76 us -> 0.1 us  [close(): jnp.where(keep_mask, total, jnp.zeros_like(total)).astype(jnp.bfloat16)]
  transfers between devices with their start and end apart: 6 -> 21, of which waited for: 4 -> 6; matrix products, arithmetic and copies ran while one was open for 1% -> 2% of each run, Pallas kernels for 0% -> 43%
where the time goes in v1:
time: 101 us; the launch traced here: 99.2 us
  Pallas kernels  42.9 us (42%)
  waiting for transfers between devices  27.5 us (27%)
  starting transfers between devices  20.9 us (21%)
  local copies, waits for them, and re-layouts  3.77 us (4%)
  other arithmetic  2.58 us (3%)
  between operations  1.58 us (2%)
    pallas_call x9, Pallas kernels, call_terms(): pl.pallas_call(functools.partial(sum_terms, slots, ways, None if before i...  42.9 us
    ppermute x21, waiting for transfers between devices, permute(): lax.ppermute(array, axis, sorted(pairs))  27.5 us
    ppermute x21, starting transfers between devices, permute(): lax.ppermute(array, axis, sorted(pairs))  20.9 us
    unnamed x10, local copies, waits for them, and re-layouts  3.66 us
  transfers between devices with their start and end apart: 21, of which 6 were waited for; matrix products, arithmetic and copies ran while one was open for 2% of the time, Pallas kernels for 43%

profile of v1, /device:TPU:25, one launch (start us, length us, event | category | flops | bytes accessed | tf_op | source)
XLA Modules:
  0.0 99.2 jit_solution(15197303972574085041)
XLA Ops:
  0.0 0.7 collective-permute-start.1
  2.1 1.1 %bitcast_select_fusion = (bf16[2,256,256]{2,1,0:T(8,128)(2,1)S(1)}, bf16[2,256,256]{2,1,0:T(8,128)(2,1)S(1)}) fusion(bf16[1,8,256,256]{3,2,1,0:T(8,128)(2,1)} %param.6, pred[256,256]{1,0:T(8,128)(4,1)S(1)} %broadcast_and_fusion), kind=kLoop, calls=%fused_computation.11 | loop fusion | flops 262144 | bytes 1114112 | tf_op jit(solution)/shard_map/jit(_where)/select_n | solution.py:227
  3.2 1.0 %collective-permute-start.3 = (bf16[2,256,256]{2,1,0:T(8,128)(2,1)S(1)}, bf16[2,256,256]{2,1,0:T(8,128)(2,1)S(1)}, u32[]{:S(2)}, u32[]{:S(2)}) collective-permute-start(bf16[2,256,256]{2,1,0:T(8,128)(2,1)S(1)} %get-tuple-element.49), channel_id=1, source_target_pairs={{0,18},{2,16},{4,22},{6,20},{8,26},{10,24},{12,30},{14,28},{16,2},... | collective-permute-start | bytes 786440 | tf_op jit(solution)/shard_map/ppermute | solution.py:166
  4.2 2.3 %collective-permute-start = (bf16[2,256,256]{2,1,0:T(8,128)(2,1)S(1)}, bf16[2,256,256]{2,1,0:T(8,128)(2,1)S(1)}, u32[]{:S(2)}, u32[]{:S(2)}) collective-permute-start(bf16[2,256,256]{2,1,0:T(8,128)(2,1)S(1)} %get-tuple-element.50), channel_id=1, source_target_pairs={{0,18},{2,16},{4,22},{6,20},{8,26},{10,24},{12,30},{14,28},{16,2},... | collective-permute-start | bytes 786440 | tf_op jit(solution)/shard_map/ppermute | solution.py:166
  6.6 1.7 %copy-done = bf16[1,20,256,256]{3,2,1,0:T(8,128)(2,1)S(1)} copy-done((bf16[1,20,256,256]{3,2,1,0:T(8,128)(2,1)S(1)}, bf16[1,20,256,256]{3,2,1,0:T(8,128)(2,1)}, u32[]{:S(2)}) %copy-start) | copy-done | bytes 2621464
  8.3 1.2 %copy-done.2 = bf16[1,8,256,256]{3,2,1,0:T(8,128)(2,1)S(1)} copy-done((bf16[1,8,256,256]{3,2,1,0:T(8,128)(2,1)S(1)}, bf16[1,8,256,256]{3,2,1,0:T(8,128)(2,1)}, u32[]{:S(2)}) %copy-start.2) | copy-done | bytes 1048600
  9.6 0.7 copy-done.3
  10.2 5.7 %shard_map.64.refs_4_ = f32[8,512,256]{2,1,0:T(8,128)S(1)} custom-call(s32[20]{0:T(128)S(1)} %copy-done.3, s32[4]{0:T(128)S(1)} %add_add_fusion.1.meta_ref, bf16[8,256,256]{2,1,0:T(8,128)(2,1)S(1)} %bitcast.31, bf16[8,256,256]{2,1,0:T(8,128)(2,1)S(1)} %collective-permute-done.1.refs_1_, bf16[1,20,512,512]{3,2,1,0:T(8,128)(2,1)} %refs_2_.17, ...), custom_call_target="tpu_custom_call" | custom-call | flops 6442450944 | bytes 2621440 | tf_op jit(solution)/shard_map/pallas_call | solution.py:150
  16.0 14.1 %collective-permute-done.refs_0_ = bf16[2,256,256]{2,1,0:T(8,128)(2,1)S(1)} collective-permute-done((bf16[2,256,256]{2,1,0:T(8,128)(2,1)S(1)}, bf16[2,256,256]{2,1,0:T(8,128)(2,1)S(1)}, u32[]{:S(2)}, u32[]{:S(2)}) %collective-permute-start) | collective-permute-done | bytes 262176 | tf_op jit(solution)/shard_map/ppermute | solution.py:166
  30.6 3.1 %collective-permute-start.2 = (bf16[2,256,256]{2,1,0:T(8,128)(2,1)S(1)}, bf16[2,256,256]{2,1,0:T(8,128)(2,1)S(1)}, u32[]{:S(2)}, u32[]{:S(2)}) collective-permute-start(bf16[2,256,256]{2,1,0:T(8,128)(2,1)S(1)} %collective-permute-done.refs_0_), channel_id=1, source_target_pairs={{0,4},{4,8},{6,2},{8,12},{10,6},{14,10},{16,20},{20,24},{22,18},{2... | collective-permute-start | bytes 786440 | tf_op jit(solution)/shard_map/ppermute | solution.py:166
  33.8 5.1 %shard_map.65.refs_4_ = f32[2,512,256]{2,1,0:T(8,128)S(1)} custom-call(s32[20]{0:T(128)S(1)} %copy-done.3, s32[4]{0:T(128)S(1)} %add_add_fusion.2.meta_ref, bf16[2,256,256]{2,1,0:T(8,128)(2,1)S(1)} %collective-permute-done.refs_0_, bf16[2,256,256]{2,1,0:T(8,128)(2,1)S(1)} %collective-permute-done.4.refs_1_, bf16[1,20,512,512]{3,2,1,0:T(8,128)(2,1)} %refs_2_.17, ...), custom_call_target="tpu_custom_call" | custom-call | flops 1610612736 | bytes 2621440 | tf_op jit(solution)/shard_map/pallas_call | solution.py:150
  39.1 1.9 %collective-permute-start.8 = (bf16[2,256,256]{2,1,0:T(8,128)(2,1)S(1)}, bf16[2,256,256]{2,1,0:T(8,128)(2,1)S(1)}, u32[]{:S(2)}, u32[]{:S(2)}) collective-permute-start(bf16[2,256,256]{2,1,0:T(8,128)(2,1)S(1)} %collective-permute-done.3.refs_0_), channel_id=1, source_target_pairs={{0,4},{4,8},{6,2},{8,12},{10,6},{14,10},{16,20},{20,24},{22,18},{2... | collective-permute-start | bytes 786440 | tf_op jit(solution)/shard_map/ppermute | solution.py:166
  41.3 0.9 collective-permute-start.6
  42.3 5.1 %shard_map.66.refs_4_ = f32[2,512,256]{2,1,0:T(8,128)S(1)} custom-call(s32[20]{0:T(128)S(1)} %copy-done.3, s32[4]{0:T(128)S(1)} %add_add_fusion.2.meta_ref, bf16[2,256,256]{2,1,0:T(8,128)(2,1)S(1)} %collective-permute-done.3.refs_0_, bf16[2,256,256]{2,1,0:T(8,128)(2,1)S(1)} %collective-permute-done.5.refs_1_, bf16[1,20,512,512]{3,2,1,0:T(8,128)(2,1)} %refs_2_.17, ...), custom_call_target="tpu_custom_call" | custom-call | flops 1610612736 | bytes 2621440 | tf_op jit(solution)/shard_map/pallas_call | solution.py:150
  47.4 4.2 %shard_map.67 = (f32[2,256,256]{2,1,0:T(8,128)S(1)}, bf16[2,256,256]{2,1,0:T(8,128)(2,1)S(1)}) custom-call(s32[20]{0:T(128)S(1)} %copy-done.3, s32[4]{0:T(128)S(1)} %add_add_fusion.meta_ref, bf16[2,256,256]{2,1,0:T(8,128)(2,1)S(1)} %collective-permute-done.2.refs_0_, bf16[2,256,256]{2,1,0:T(8,128)(2,1)S(1)} %collective-permute-done.6.refs_1_, ...), custom_call_target="tpu_custom_call" | custom-call | flops 1610612736 | bytes 2621440 | tf_op jit(solution)/shard_map/pallas_call | solution.py:150
  51.6 6.0 %collective-permute-done.9.refs_0_ = bf16[2,256,256]{2,1,0:T(8,128)(2,1)S(1)} collective-permute-done((bf16[2,256,256]{2,1,0:T(8,128)(2,1)S(1)}, bf16[2,256,256]{2,1,0:T(8,128)(2,1)S(1)}, u32[]{:S(2)}, u32[]{:S(2)}) %collective-permute-start.9) | collective-permute-done | bytes 262176 | tf_op jit(solution)/shard_map/ppermute | solution.py:166
  57.6 0.8 collective-permute-start.10
  58.4 2.2 %collective-permute-start.13 = (bf16[2,256,256]{2,1,0:T(8,128)(2,1)S(1)}, bf16[2,256,256]{2,1,0:T(8,128)(2,1)S(1)}, u32[]{:S(2)}, u32[]{:S(2)}) collective-permute-start(bf16[2,256,256]{2,1,0:T(8,128)(2,1)S(1)} %collective-permute-done.9.refs_0_), channel_id=1, source_target_pairs={{0,4},{4,8},{6,2},{8,12},{10,6},{14,10},{16,20},{20,24},{22,18},{2... | collective-permute-start | bytes 786440 | tf_op jit(solution)/shard_map/ppermute | solution.py:166
  60.7 0.8 collective-permute-start.7
  61.5 5.1 %shard_map.68.refs_4_ = f32[2,512,256]{2,1,0:T(8,128)S(1)} custom-call(s32[20]{0:T(128)S(1)} %copy-done.3, s32[4]{0:T(128)S(1)} %add_add_fusion.2.meta_ref, bf16[2,256,256]{2,1,0:T(8,128)(2,1)S(1)} %collective-permute-done.9.refs_0_, bf16[2,256,256]{2,1,0:T(8,128)(2,1)S(1)} %collective-permute-done.10.refs_1_, bf16[1,20,512,512]{3,2,1,0:T(8,128)(2,1)} %refs_2_.17, ...), custom_call_target="tpu_custom_call" | custom-call | flops 1610612736 | bytes 2621440 | tf_op jit(solution)/shard_map/pallas_call | solution.py:150
  66.6 4.2 %shard_map.69 = (f32[2,256,256]{2,1,0:T(8,128)S(1)}, bf16[2,256,256]{2,1,0:T(8,128)(2,1)S(1)}) custom-call(s32[20]{0:T(128)S(1)} %copy-done.3, s32[4]{0:T(128)S(1)} %add_add_fusion.meta_ref, bf16[2,256,256]{2,1,0:T(8,128)(2,1)S(1)} %collective-permute-done.8.refs_0_, bf16[2,256,256]{2,1,0:T(8,128)(2,1)S(1)} %collective-permute-done.11.refs_1_, ...), custom_call_target="tpu_custom_call" | custom-call | flops 1610612736 | bytes 2621440 | tf_op jit(solution)/shard_map/pallas_call | solution.py:150
  70.8 0.8 collective-permute-done.14.refs_0_
  71.6 3.3 %collective-permute-start.18 = (bf16[2,256,256]{2,1,0:T(8,128)(2,1)S(1)}, bf16[2,256,256]{2,1,0:T(8,128)(2,1)S(1)}, u32[]{:S(2)}, u32[]{:S(2)}) collective-permute-start(bf16[2,256,256]{2,1,0:T(8,128)(2,1)S(1)} %collective-permute-done.14.refs_0_), channel_id=1, source_target_pairs={{0,4},{4,8},{6,2},{8,12},{10,6},{14,10},{16,20},{20,24},{22,18},{2... | collective-permute-start | bytes 786440 | tf_op jit(solution)/shard_map/ppermute | solution.py:166
  75.0 0.8 collective-permute-start.15
  76.5 5.3 %collective-permute-done.18.refs_0_ = bf16[2,256,256]{2,1,0:T(8,128)(2,1)S(1)} collective-permute-done((bf16[2,256,256]{2,1,0:T(8,128)(2,1)S(1)}, bf16[2,256,256]{2,1,0:T(8,128)(2,1)S(1)}, u32[]{:S(2)}, u32[]{:S(2)}) %collective-permute-start.18) | collective-permute-done | bytes 262176 | tf_op jit(solution)/shard_map/ppermute | solution.py:166
  81.8 1.3 %collective-permute-start.19 = (bf16[2,256,256]{2,1,0:T(8,128)(2,1)S(1)}, bf16[2,256,256]{2,1,0:T(8,128)(2,1)S(1)}, u32[]{:S(2)}, u32[]{:S(2)}) collective-permute-start(bf16[2,256,256]{2,1,0:T(8,128)(2,1)S(1)} %collective-permute-done.18.refs_0_), channel_id=1, source_target_pairs={{0,1},{1,0},{2,3},{3,2},{4,5},{5,4},{6,7},{7,6},{8,9},{9,8},{10,11... | collective-permute-start | bytes 786440 | tf_op jit(solution)/shard_map/ppermute | solution.py:166
  83.2 5.1 %shard_map.70.refs_4_ = f32[2,512,256]{2,1,0:T(8,128)S(1)} custom-call(s32[20]{0:T(128)S(1)} %copy-done.3, s32[4]{0:T(128)S(1)} %add_add_fusion.2.meta_ref, bf16[2,256,256]{2,1,0:T(8,128)(2,1)S(1)} %collective-permute-done.14.refs_0_, bf16[2,256,256]{2,1,0:T(8,128)(2,1)S(1)} %collective-permute-done.15.refs_1_, bf16[1,20,512,512]{3,2,1,0:T(8,128)(2,1)} %refs_2_.17, ...), custom_call_target="tpu_custom_call" | custom-call | flops 1610612736 | bytes 2621440 | tf_op jit(solution)/shard_map/pallas_call | solution.py:150
  88.3 4.2 %shard_map.71 = (f32[2,256,256]{2,1,0:T(8,128)S(1)}, bf16[2,256,256]{2,1,0:T(8,128)(2,1)S(1)}) custom-call(s32[20]{0:T(128)S(1)} %copy-done.3, s32[4]{0:T(128)S(1)} %add_add_fusion.meta_ref, bf16[2,256,256]{2,1,0:T(8,128)(2,1)S(1)} %collective-permute-done.13.refs_0_, bf16[2,256,256]{2,1,0:T(8,128)(2,1)S(1)} %collective-permute-done.16.refs_1_, ...), custom_call_target="tpu_custom_call" | custom-call | flops 1610612736 | bytes 2621440 | tf_op jit(solution)/shard_map/pallas_call | solution.py:150
  92.6 4.2 %shard_map.72 = (f32[2,256,256]{2,1,0:T(8,128)S(1)}, bf16[2,256,256]{2,1,0:T(8,128)(2,1)S(1)}) custom-call(s32[20]{0:T(128)S(1)} %copy-done.3, s32[4]{0:T(128)S(1)} %add_add_fusion.meta_ref, bf16[2,256,256]{2,1,0:T(8,128)(2,1)S(1)} %collective-permute-done.18.refs_0_, bf16[2,256,256]{2,1,0:T(8,128)(2,1)S(1)} %collective-permute-done.19.refs_1_, ...), custom_call_target="tpu_custom_call" | custom-call | flops 1610612736 | bytes 2621440 | tf_op jit(solution)/shard_map/pallas_call | solution.py:150
  96.7 0.5 collective-permute-start.20
  97.5 0.9 collective-permute-done.20
  98.4 0.8 fusion.5
  (42 shorter events, 2.3 us)
Async XLA Ops:
  0.0 6.6 %collective-permute-start.1 = (bf16[8,256,256]{2,1,0:T(8,128)(2,1)}, bf16[8,256,256]{2,1,0:T(8,128)(2,1)S(1)}, u32[]{:S(2)}, u32[]{:S(2)}) collective-permute-start(bf16[8,256,256]{2,1,0:T(8,128)(2,1)} %bitcast.30), channel_id=1, source_target_pairs={{0,1},{1,0},{2,3},{3,2},{4,5},{5,4},{6,7},{7,6},{8,9},{9,8},{10,11... | collective-permute-start | bytes 3145736 | tf_op jit(solution)/shard_map/ppermute | solution.py:166
  3.2 35.8 %collective-permute-start.3 = (bf16[2,256,256]{2,1,0:T(8,128)(2,1)S(1)}, bf16[2,256,256]{2,1,0:T(8,128)(2,1)S(1)}, u32[]{:S(2)}, u32[]{:S(2)}) collective-permute-start(bf16[2,256,256]{2,1,0:T(8,128)(2,1)S(1)} %get-tuple-element.49), channel_id=1, source_target_pairs={{0,18},{2,16},{4,22},{6,20},{8,26},{10,24},{12,30},{14,28},{16,2},... | collective-permute-start | bytes 786440 | tf_op jit(solution)/shard_map/ppermute | solution.py:166
  4.2 25.8 %collective-permute-start = (bf16[2,256,256]{2,1,0:T(8,128)(2,1)S(1)}, bf16[2,256,256]{2,1,0:T(8,128)(2,1)S(1)}, u32[]{:S(2)}, u32[]{:S(2)}) collective-permute-start(bf16[2,256,256]{2,1,0:T(8,128)(2,1)S(1)} %get-tuple-element.50), channel_id=1, source_target_pairs={{0,18},{2,16},{4,22},{6,20},{8,26},{10,24},{12,30},{14,28},{16,2},... | collective-permute-start | bytes 786440 | tf_op jit(solution)/shard_map/ppermute | solution.py:166
  6.6 1.7 %copy-start = (bf16[1,20,256,256]{3,2,1,0:T(8,128)(2,1)S(1)}, bf16[1,20,256,256]{3,2,1,0:T(8,128)(2,1)}, u32[]{:S(2)}) copy-start(bf16[1,20,256,256]{3,2,1,0:T(8,128)(2,1)} %refs_3_.17) | copy-start | bytes 7864324
  8.3 1.2 %copy-start.2 = (bf16[1,8,256,256]{3,2,1,0:T(8,128)(2,1)S(1)}, bf16[1,8,256,256]{3,2,1,0:T(8,128)(2,1)}, u32[]{:S(2)}) copy-start(bf16[1,8,256,256]{3,2,1,0:T(8,128)(2,1)} %param.6) | copy-start | bytes 3145732
  9.6 0.7 copy-start.3
  10.2 23.6 %copy-start.1 = (bf16[1,20,256,256]{3,2,1,0:T(8,128)(2,1)S(1)}, bf16[1,20,256,256]{3,2,1,0:T(8,128)(2,1)}, u32[]{:S(2)}) copy-start(bf16[1,20,256,256]{3,2,1,0:T(8,128)(2,1)} %refs_3_.17) | copy-start | bytes 7864324
  30.1 3.7 %collective-permute-start.4 = (bf16[2,256,256]{2,1,0:T(8,128)(2,1)S(1)}, bf16[2,256,256]{2,1,0:T(8,128)(2,1)S(1)}, u32[]{:S(2)}, u32[]{:S(2)}) collective-permute-start(bf16[2,256,256]{2,1,0:T(8,128)(2,1)S(1)} %collective-permute-done.refs_0_), channel_id=1, source_target_pairs={{0,1},{1,0},{2,3},{3,2},{4,5},{5,4},{6,7},{7,6},{8,9},{9,8},{10,11... | collective-permute-start | bytes 786440 | tf_op jit(solution)/shard_map/ppermute | solution.py:166
  30.6 10.6 %collective-permute-start.2 = (bf16[2,256,256]{2,1,0:T(8,128)(2,1)S(1)}, bf16[2,256,256]{2,1,0:T(8,128)(2,1)S(1)}, u32[]{:S(2)}, u32[]{:S(2)}) collective-permute-start(bf16[2,256,256]{2,1,0:T(8,128)(2,1)S(1)} %collective-permute-done.refs_0_), channel_id=1, source_target_pairs={{0,4},{4,8},{6,2},{8,12},{10,6},{14,10},{16,20},{20,24},{22,18},{2... | collective-permute-start | bytes 786440 | tf_op jit(solution)/shard_map/ppermute | solution.py:166
  38.9 3.3 %collective-permute-start.5 = (bf16[2,256,256]{2,1,0:T(8,128)(2,1)S(1)}, bf16[2,256,256]{2,1,0:T(8,128)(2,1)S(1)}, u32[]{:S(2)}, u32[]{:S(2)}) collective-permute-start(bf16[2,256,256]{2,1,0:T(8,128)(2,1)S(1)} %collective-permute-done.3.refs_0_), channel_id=1, source_target_pairs={{0,1},{1,0},{2,3},{3,2},{4,5},{5,4},{6,7},{7,6},{8,9},{9,8},{10,11... | collective-permute-start | bytes 786440 | tf_op jit(solution)/shard_map/ppermute | solution.py:166
  39.1 19.3 %collective-permute-start.8 = (bf16[2,256,256]{2,1,0:T(8,128)(2,1)S(1)}, bf16[2,256,256]{2,1,0:T(8,128)(2,1)S(1)}, u32[]{:S(2)}, u32[]{:S(2)}) collective-permute-start(bf16[2,256,256]{2,1,0:T(8,128)(2,1)S(1)} %collective-permute-done.3.refs_0_), channel_id=1, source_target_pairs={{0,4},{4,8},{6,2},{8,12},{10,6},{14,10},{16,20},{20,24},{22,18},{2... | collective-permute-start | bytes 786440 | tf_op jit(solution)/shard_map/ppermute | solution.py:166
  41.3 6.1 %collective-permute-start.6 = (bf16[2,256,256]{2,1,0:T(8,128)(2,1)S(1)}, bf16[2,256,256]{2,1,0:T(8,128)(2,1)S(1)}, u32[]{:S(2)}, u32[]{:S(2)}) collective-permute-start(bf16[2,256,256]{2,1,0:T(8,128)(2,1)S(1)} %collective-permute-done.2.refs_0_), channel_id=1, source_target_pairs={{0,1},{1,0},{2,3},{3,2},{4,5},{5,4},{6,7},{7,6},{8,9},{9,8},{10,11... | collective-permute-start | bytes 786440 | tf_op jit(solution)/shard_map/ppermute | solution.py:166
  42.2 15.4 %collective-permute-start.9 = (bf16[2,256,256]{2,1,0:T(8,128)(2,1)S(1)}, bf16[2,256,256]{2,1,0:T(8,128)(2,1)S(1)}, u32[]{:S(2)}, u32[]{:S(2)}) collective-permute-start(bf16[2,256,256]{2,1,0:T(8,128)(2,1)S(1)} %get-tuple-element.54), channel_id=1, source_target_pairs={{0,18},{2,16},{4,22},{6,20},{8,26},{10,24},{12,30},{14,28},{16,2},... | collective-permute-start | bytes 786440 | tf_op jit(solution)/shard_map/ppermute | solution.py:166
  57.6 3.9 %collective-permute-start.10 = (bf16[2,256,256]{2,1,0:T(8,128)(2,1)S(1)}, bf16[2,256,256]{2,1,0:T(8,128)(2,1)S(1)}, u32[]{:S(2)}, u32[]{:S(2)}) collective-permute-start(bf16[2,256,256]{2,1,0:T(8,128)(2,1)S(1)} %collective-permute-done.9.refs_0_), channel_id=1, source_target_pairs={{0,1},{1,0},{2,3},{3,2},{4,5},{5,4},{6,7},{7,6},{8,9},{9,8},{10,11... | collective-permute-start | bytes 786440 | tf_op jit(solution)/shard_map/ppermute | solution.py:166
  58.4 8.2 %collective-permute-start.11 = (bf16[2,256,256]{2,1,0:T(8,128)(2,1)S(1)}, bf16[2,256,256]{2,1,0:T(8,128)(2,1)S(1)}, u32[]{:S(2)}, u32[]{:S(2)}) collective-permute-start(bf16[2,256,256]{2,1,0:T(8,128)(2,1)S(1)} %collective-permute-done.8.refs_0_), channel_id=1, source_target_pairs={{0,1},{1,0},{2,3},{3,2},{4,5},{5,4},{6,7},{7,6},{8,9},{9,8},{10,11... | collective-permute-start | bytes 786440 | tf_op jit(solution)/shard_map/ppermute | solution.py:166
  58.4 13.3 %collective-permute-start.14 = (bf16[2,256,256]{2,1,0:T(8,128)(2,1)S(1)}, bf16[2,256,256]{2,1,0:T(8,128)(2,1)S(1)}, u32[]{:S(2)}, u32[]{:S(2)}) collective-permute-start(bf16[2,256,256]{2,1,0:T(8,128)(2,1)S(1)} %get-tuple-element.53), channel_id=1, source_target_pairs={{0,18},{2,16},{4,22},{6,20},{8,26},{10,24},{12,30},{14,28},{16,2},... | collective-permute-start | bytes 786440 | tf_op jit(solution)/shard_map/ppermute | solution.py:166
  58.4 17.5 %collective-permute-start.13 = (bf16[2,256,256]{2,1,0:T(8,128)(2,1)S(1)}, bf16[2,256,256]{2,1,0:T(8,128)(2,1)S(1)}, u32[]{:S(2)}, u32[]{:S(2)}) collective-permute-start(bf16[2,256,256]{2,1,0:T(8,128)(2,1)S(1)} %collective-permute-done.9.refs_0_), channel_id=1, source_target_pairs={{0,4},{4,8},{6,2},{8,12},{10,6},{14,10},{16,20},{20,24},{22,18},{2... | collective-permute-start | bytes 786440 | tf_op jit(solution)/shard_map/ppermute | solution.py:166
  60.7 15.7 %collective-permute-start.7 = (bf16[2,256,256]{2,1,0:T(8,128)(2,1)S(1)}, bf16[2,256,256]{2,1,0:T(8,128)(2,1)S(1)}, u32[]{:S(2)}, u32[]{:S(2)}) collective-permute-start(bf16[2,256,256]{2,1,0:T(8,128)(2,1)S(1)} %get-tuple-element.32), channel_id=1, source_target_pairs={{0,1},{1,0},{2,3},{3,2},{4,5},{5,4},{6,7},{7,6},{8,9},{9,8},{10,11... | collective-permute-start | bytes 786440 | tf_op jit(solution)/shard_map/ppermute | solution.py:166
  71.6 10.2 %collective-permute-start.18 = (bf16[2,256,256]{2,1,0:T(8,128)(2,1)S(1)}, bf16[2,256,256]{2,1,0:T(8,128)(2,1)S(1)}, u32[]{:S(2)}, u32[]{:S(2)}) collective-permute-start(bf16[2,256,256]{2,1,0:T(8,128)(2,1)S(1)} %collective-permute-done.14.refs_0_), channel_id=1, source_target_pairs={{0,4},{4,8},{6,2},{8,12},{10,6},{14,10},{16,20},{20,24},{22,18},{2... | collective-permute-start | bytes 786440 | tf_op jit(solution)/shard_map/ppermute | solution.py:166
  75.0 8.2 %collective-permute-start.15 = (bf16[2,256,256]{2,1,0:T(8,128)(2,1)S(1)}, bf16[2,256,256]{2,1,0:T(8,128)(2,1)S(1)}, u32[]{:S(2)}, u32[]{:S(2)}) collective-permute-start(bf16[2,256,256]{2,1,0:T(8,128)(2,1)S(1)} %collective-permute-done.14.refs_0_), channel_id=1, source_target_pairs={{0,1},{1,0},{2,3},{3,2},{4,5},{5,4},{6,7},{7,6},{8,9},{9,8},{10,11... | collective-permute-start | bytes 786440 | tf_op jit(solution)/shard_map/ppermute | solution.py:166
  75.8 21.4 %collective-permute-start.12 = (bf16[2,256,256]{2,1,0:T(8,128)(2,1)S(1)}, bf16[2,256,256]{2,1,0:T(8,128)(2,1)S(1)}, u32[]{:S(2)}, u32[]{:S(2)}) collective-permute-start(bf16[2,256,256]{2,1,0:T(8,128)(2,1)S(1)} %get-tuple-element.38), channel_id=1, source_target_pairs={{0,1},{1,0},{2,3},{3,2},{4,5},{5,4},{6,7},{7,6},{8,9},{9,8},{10,11... | collective-permute-start | bytes 786440 | tf_op jit(solution)/shard_map/ppermute | solution.py:166
  75.9 12.4 %collective-permute-start.16 = (bf16[2,256,256]{2,1,0:T(8,128)(2,1)S(1)}, bf16[2,256,256]{2,1,0:T(8,128)(2,1)S(1)}, u32[]{:S(2)}, u32[]{:S(2)}) collective-permute-start(bf16[2,256,256]{2,1,0:T(8,128)(2,1)S(1)} %collective-permute-done.13.refs_0_), channel_id=1, source_target_pairs={{0,1},{1,0},{2,3},{3,2},{4,5},{5,4},{6,7},{7,6},{8,9},{9,8},{10,11... | collective-permute-start | bytes 786440 | tf_op jit(solution)/shard_map/ppermute | solution.py:166
  81.8 10.7 %collective-permute-start.19 = (bf16[2,256,256]{2,1,0:T(8,128)(2,1)S(1)}, bf16[2,256,256]{2,1,0:T(8,128)(2,1)S(1)}, u32[]{:S(2)}, u32[]{:S(2)}) collective-permute-start(bf16[2,256,256]{2,1,0:T(8,128)(2,1)S(1)} %collective-permute-done.18.refs_0_), channel_id=1, source_target_pairs={{0,1},{1,0},{2,3},{3,2},{4,5},{5,4},{6,7},{7,6},{8,9},{9,8},{10,11... | collective-permute-start | bytes 786440 | tf_op jit(solution)/shard_map/ppermute | solution.py:166
  92.5 4.9 %collective-permute-start.17 = (bf16[2,256,256]{2,1,0:T(8,128)(2,1)S(1)}, bf16[2,256,256]{2,1,0:T(8,128)(2,1)S(1)}, u32[]{:S(2)}, u32[]{:S(2)}) collective-permute-start(bf16[2,256,256]{2,1,0:T(8,128)(2,1)S(1)} %get-tuple-element.44), channel_id=1, source_target_pairs={{0,1},{1,0},{2,3},{3,2},{4,5},{5,4},{6,7},{7,6},{8,9},{9,8},{10,11... | collective-permute-start | bytes 786440 | tf_op jit(solution)/shard_map/ppermute | solution.py:166
  96.7 1.7 %collective-permute-start.20 = (bf16[2,256,256]{2,1,0:T(8,128)(2,1)S(1)}, bf16[2,256,256]{2,1,0:T(8,128)(2,1)S(1)}, u32[]{:S(2)}, u32[]{:S(2)}) collective-permute-start(bf16[2,256,256]{2,1,0:T(8,128)(2,1)S(1)} %get-tuple-element.48), channel_id=1, source_target_pairs={{0,1},{1,0},{2,3},{3,2},{4,5},{5,4},{6,7},{7,6},{8,9},{9,8},{10,11... | collective-permute-start | bytes 786440 | tf_op jit(solution)/shard_map/ppermute | solution.py:166
  97.4 1.0 copy-start.4

commit v2 on v1

v2 whole, which is shorter than its diff:
```python
import functools

import jax
import jax.numpy as jnp
from jax import lax
from jax.experimental import pallas as pl
from jax.experimental.pallas import tpu as pltpu
from jax.sharding import PartitionSpec as P

SPINS = 8
CLASSES = 5
SPARE = 0
VMEM = 40 * 2**20
WHOLE_VMEM = 62 * 2**20
RUNS = (4, 4)
PLACE, LEFT, RIGHT, LIVE, OWN = 0, 1, 2, 3, 3 + CLASSES
HINT = pl.CostEstimate(flops=10**6, bytes_accessed=10**3, transcendentals=0)


def sharing(shift_ref, meta_ref, terms, ways, spare):
    both = terms * ways // CLASSES
    half = both // 2

    def tally(term, counts):
        return tuple(n + (shift_ref[term] == c).astype(jnp.int32) for c, n in enumerate(counts))

    counts = lax.fori_loop(0, terms, tally, (jnp.int32(0),) * CLASSES)
    given_before, taken_before, plan = jnp.int32(0), jnp.int32(0), []
    for c, count in enumerate(counts):
        live = meta_ref[LIVE + c]
        surplus = jnp.maximum(count - half, 0) * live
        lack = jnp.maximum(both - half - (count if both % 2 == 0 else count), 0) * live
        given = jnp.clip(spare - given_before, 0, surplus)
        taken = jnp.clip(spare - taken_before, 0, lack)
        plan.append((count - given, given_before, given, taken_before, taken))
        given_before, taken_before = given_before + surplus, taken_before + lack
    return plan


def chosen(plan, shift_class, entry):
    value = jnp.int32(0)
    for c, entries in enumerate(plan):
        value = jnp.where(shift_class == c, entries[entry], value)
    return value


def pack_terms(spare, ways, shift_ref, meta_ref, left_ref, right_ref, _, lefts, rights, left_sem, right_sem):
    terms = shift_ref.shape[0]
    plan = sharing(shift_ref, meta_ref, terms, ways, spare)

    def copies(term, slot):
        return (
            pltpu.make_async_copy(left_ref.at[0, term], lefts.at[slot], left_sem.at[slot]),
            pltpu.make_async_copy(right_ref.at[0, term], rights.at[slot], right_sem.at[slot]),
        )

    def step(term, ranks):
        c = shift_ref[term]
        rank = jnp.int32(0)
        for number, seen in enumerate(ranks):
            rank = jnp.where(c == number, seen, rank)
        beyond = rank - chosen(plan, c, 0)
        slot = chosen(plan, c, 1) + beyond

        @pl.when((beyond >= 0) & (beyond < chosen(plan, c, 2)))
        def _():
            for copy in copies(term, slot):
                copy.start()

        return tuple(seen + (c == number).astype(jnp.int32) for number, seen in enumerate(ranks))

    lax.fori_loop(0, terms, step, (jnp.int32(0),) * CLASSES)
    total = jnp.int32(0)
    for entries in plan:
        total += entries[2]

    @pl.loop(0, total)
    def _(slot):
        for copy in copies(0, slot):
            copy.wait()


def call_pack(shift, meta, left, right, ways, tick):
    smem, vmem = pl.BlockSpec(memory_space=pltpu.SMEM), pl.BlockSpec(memory_space=pltpu.VMEM)
    return pl.pallas_call(
        functools.partial(pack_terms, SPARE, ways),
        out_shape=[jax.ShapeDtypeStruct((SPARE, *array.shape[2:]), array.dtype) for array in (left, right)],
        in_specs=[smem, smem] + [pl.BlockSpec(memory_space=pl.ANY)] * 3,
        out_specs=[vmem, vmem],
        scratch_shapes=[pltpu.SemaphoreType.DMA((SPARE,)), pltpu.SemaphoreType.DMA((SPARE,))],
        compiler_params=pltpu.CompilerParams(vmem_limit_bytes=WHOLE_VMEM),
        cost_estimate=HINT,
    )(shift, meta, left, right, tick)


def sum_terms(kinds, ways, slots, pieces, outs, extras, ticks, resume, finish, mask, group, shift_ref, meta_ref, *refs):
    kind_parts = []
    for _ in kinds:
        kind_parts.append(refs[: ways * pieces])
        refs = refs[ways * pieces :]
    left_ref, right_ref, refs = refs[0], refs[1], refs[2:]
    if extras:
        extra_left_ref, extra_right_ref, refs = refs[0], refs[1], refs[2:]
    refs = refs[ticks:]
    if resume:
        before_ref, refs = refs[0], refs[1:]
    if finish:
        keep_ref, give_refs, refs = refs[0], refs[1:ways], refs[ways:]
    else:
        out_refs, refs = refs[:outs], refs[outs:]
    token_ref, left_buf, right_buf, source, applied, refs = *refs[:5], refs[5:]
    if finish or outs > 1:
        total, refs = refs[0], refs[1:]
    else:
        total = out_refs[0]
    left_sem, right_sem, part_sem, before_sem = refs
    place = meta_ref[PLACE]
    vectors = source.shape[1]
    _, share, columns = kind_parts[0][0].shape
    rows = share * ways
    widths = [kind_parts[0][piece * ways].shape[0] for piece in range(pieces)]

    def copy_parts(kind):
        for piece, width in enumerate(widths):
            for turn in range(ways):
                row = pl.multiple_of(lax.rem(place + ways - turn, ways) * share, share)
                yield pltpu.make_async_copy(
                    kind_parts[kind][piece * ways + turn],
                    source.at[kind, pl.ds(sum(widths[:piece]), width), pl.ds(row, share), :],
                    part_sem.at[kind, piece * ways + turn],
                )

    def copies(term, slot, lefts=left_ref.at[0], rights=right_ref.at[0]):
        return (
            pltpu.make_async_copy(lefts.at[term], left_buf.at[slot], left_sem.at[slot]),
            pltpu.make_async_copy(rights.at[term], right_buf.at[slot], right_sem.at[slot]),
        )

    for copy in copy_parts(0):
        copy.start()
    plan = sharing(shift_ref, meta_ref, shift_ref.shape[0], ways, SPARE) if extras else None
    counts = []
    for kind, position in enumerate(kinds):
        shift_class = jnp.int32(0) if position is None else meta_ref[position]
        kept = jnp.minimum(chosen(plan, shift_class, 0), slots) if extras else slots

        def fetch(term, count):
            hit = (shift_ref[term] == shift_class) & (count < kept)

            @pl.when(hit)
            def _():
                for copy in copies(term, kind * slots + count):
                    copy.start()

            return count + hit.astype(jnp.int32)

        count = lax.fori_loop(0, shift_ref.shape[0], fetch, jnp.int32(0))
        if extras:
            first = chosen(plan, shift_class, 3)
            more = jnp.minimum(chosen(plan, shift_class, 4), slots - count)

            @pl.loop(0, more)
            def _(turn):
                for copy in copies(first + turn, kind * slots + count + turn, extra_left_ref, extra_right_ref):
                    copy.start()

            count = count + more
        counts.append(count)
        if kind == 0:
            if resume:
                copy_before = pltpu.make_async_copy(before_ref, total, before_sem)
                copy_before.start()
            for later in range(1, len(kinds)):
                for copy in copy_parts(later):
                    copy.start()

    token_ref[...] = jnp.zeros_like(token_ref)
    if resume:
        copy_before.wait()
    else:
        total[...] = jnp.zeros_like(total)

    def arrive(slot):
        for copy in copies(0, slot):
            copy.wait()

    def add_terms(kind, first, number):
        rights = jnp.concatenate([right_buf[first + i] for i in range(number)], axis=1)
        for vector in range(vectors):
            for i in range(number):
                applied[vector, :, i * columns : (i + 1) * columns] = jnp.dot(
                    left_buf[first + i], source[kind, vector], preferred_element_type=jnp.float32
                ).astype(jnp.bfloat16)
        width = number * columns
        total[...] += lax.dot_general(
            applied[:, :, :width].reshape(vectors * rows, width),
            rights,
            (((1,), (1,)), ((), ())),
            preferred_element_type=jnp.float32,
        ).reshape(total.shape)

    for kind in range(len(kinds)):
        for copy in copy_parts(kind):
            copy.wait()
        if mask:
            kept_rows = lax.broadcasted_iota(jnp.int32, (rows, columns), 0) < meta_ref[LEFT]
            kept_block = kept_rows & (lax.broadcasted_iota(jnp.int32, (rows, columns), 1) < meta_ref[RIGHT])
            for vector in range(vectors):
                block = source[kind, vector]
                source[kind, vector] = jnp.where(kept_block, block, jnp.zeros_like(block))
        base = kind * slots
        whole = counts[kind] // group

        @pl.loop(0, whole)
        def _(turn):
            for i in range(group):
                arrive(base + turn * group + i)
            add_terms(kind, base + turn * group, group)

        if group > 1:

            @pl.loop(whole * group, counts[kind])
            def _(slot):
                arrive(base + slot)
                add_terms(kind, base + slot, 1)

    if finish:
        for turn in range(ways):
            row = pl.multiple_of(lax.rem(place + turn, ways) * share, share)
            block = total[:, pl.ds(row, share), :]
            if turn == 0:
                keep_ref[...] = block
            else:
                give_refs[turn - 1][...] = block.astype(jnp.bfloat16)
    elif outs > 1:
        for number, out_ref in enumerate(out_refs):
            begin = sum(out.shape[0] for out in out_refs[:number])
            out_ref[...] = total[pl.ds(begin, out_ref.shape[0])]


def call_terms(shift, meta, kinds, sources, left, right, extras=(), ticks=(), before=None, finish=False, mask=False, split=None):
    ways = len(sources[0][0])
    _, share, columns = sources[0][0][0].shape
    vectors = sum(parts[0].shape[0] for parts in sources[0])
    split = split or [vectors]
    rows = share * ways
    terms = left.shape[1]
    slots = min(terms, terms * ways // CLASSES)
    group = 1 if vectors >= 4 else 2
    any_spec = pl.BlockSpec(memory_space=pl.ANY)
    smem = pl.BlockSpec(memory_space=pltpu.SMEM)
    vmem = pl.BlockSpec(memory_space=pltpu.VMEM)
    parts = [part for pieces in sources for run in pieces for part in run]
    operands = [shift, meta, *parts, left, right, *extras, *ticks]
    if before is not None:
        operands.append(before)
    scratch = [
        pltpu.VMEM((len(kinds) * slots, rows, rows), jnp.bfloat16),
        pltpu.VMEM((len(kinds) * slots, columns, columns), jnp.bfloat16),
        pltpu.VMEM((len(kinds), vectors, rows, columns), jnp.bfloat16),
        pltpu.VMEM((vectors, rows, group * columns), jnp.bfloat16),
    ]
    if finish:
        out_shape = [jax.ShapeDtypeStruct((vectors, share, columns), jnp.float32)] + [
            jax.ShapeDtypeStruct((vectors, share, columns), jnp.bfloat16)
        ] * (ways - 1)
    else:
        out_shape = [jax.ShapeDtypeStruct((width, rows, columns), jnp.float32) for width in split]
    out_shape.append(jax.ShapeDtypeStruct((8, 128), jnp.int32))
    if finish or len(split) > 1:
        scratch.append(pltpu.VMEM((vectors, rows, columns), jnp.float32))
    scratch += [
        pltpu.SemaphoreType.DMA((len(kinds) * slots,)),
        pltpu.SemaphoreType.DMA((len(kinds) * slots,)),
        pltpu.SemaphoreType.DMA((len(kinds), ways * len(sources[0]))),
        pltpu.SemaphoreType.DMA,
    ]
    return pl.pallas_call(
        functools.partial(
            sum_terms, kinds, ways, slots, len(sources[0]), len(split), bool(extras), len(ticks),
            before is not None, finish, mask, group,
        ),
        out_shape=out_shape,
        in_specs=[smem, smem] + [any_spec] * (len(operands) - 2),
        out_specs=[vmem] * len(out_shape),
        scratch_shapes=scratch,
        compiler_params=pltpu.CompilerParams(vmem_limit_bytes=WHOLE_VMEM if mask else VMEM),
        cost_estimate=HINT,
    )(*operands)


def mask_rows(starts, meta_ref, source_ref, *refs):
    outs, (buffer, sem) = refs[:-2], refs[-2:]
    share, columns = source_ref.shape[2:]
    copy = pltpu.make_async_copy(source_ref.at[0], buffer, sem)
    copy.start()
    copy.wait()
    row = meta_ref[PLACE] * share + lax.broadcasted_iota(jnp.int32, (share, columns), 0)
    kept = (row < meta_ref[LEFT]) & (lax.broadcasted_iota(jnp.int32, (share, columns), 1) < meta_ref[RIGHT])
    for start, out in zip(starts, outs):
        for vector in range(out.shape[0]):
            block = buffer[start + vector]
            out[vector] = jnp.where(kept, block, jnp.zeros_like(block))


def call_mask(meta, wavefunction, starts, widths):
    share, columns = wavefunction.shape[2:]
    return pl.pallas_call(
        functools.partial(mask_rows, starts),
        out_shape=[jax.ShapeDtypeStruct((width, share, columns), wavefunction.dtype) for width in widths],
        in_specs=[pl.BlockSpec(memory_space=pltpu.SMEM), pl.BlockSpec(memory_space=pl.ANY)],
        out_specs=[pl.BlockSpec(memory_space=pltpu.VMEM)] * len(widths),
        scratch_shapes=[pltpu.VMEM(wavefunction.shape[1:], wavefunction.dtype), pltpu.SemaphoreType.DMA],
        compiler_params=pltpu.CompilerParams(vmem_limit_bytes=VMEM),
        cost_estimate=HINT,
    )(meta, wavefunction)


def permute(array, axis, pairs):
    return lax.ppermute(array, axis, sorted(pairs)) if pairs else jnp.zeros_like(array)


def around(array):
    ways = lax.axis_size("mpo")
    return [array] + [
        permute(array, "mpo", [(i, (i + turn) % ways) for i in range(ways)]) for turn in range(1, ways)
    ]


def after(array, tick):
    return lax.optimization_barrier((array, tick))


def per_device(wavefunction, left_env, right_env, left_dims, right_dims, term_shift):
    vectors, share, columns = wavefunction.shape[1:]
    place = lax.axis_index("mpo")
    ways = lax.axis_size("mpo")
    sector = lax.axis_index("sec")
    lines = lax.axis_size("sec") // SPINS
    line, spin = sector // SPINS, sector % SPINS
    odd = spin % 2 == 1
    row_ids = place * share + jnp.arange(share, dtype=jnp.int32)
    column_ids = jnp.arange(columns, dtype=jnp.int32)
    keep_mask = ((row_ids[:, None] < left_dims[0]) & (column_ids[None, :] < right_dims[0]))[None]

    def cross(step):
        return [
            (n * SPINS + p, (n + step) * SPINS + (p ^ 1))
            for n in range(lines)
            for p in range(SPINS)
            if 0 <= n + step < lines
        ]

    relay = [
        (n * SPINS + p, n * SPINS + p + (-2 if p % 2 else 2))
        for n in range(lines)
        for p in range(SPINS)
        if 0 <= p + (-2 if p % 2 else 2) < SPINS
    ]
    relay_here = jnp.where(odd, spin + 2 < SPINS, spin >= 2)
    from_below = (jnp.where(odd, 1, 3), jnp.where(odd, 3, 1), line > 0)
    from_above = (jnp.where(odd, 4, 2), jnp.where(odd, 2, 4), line + 1 < lines)
    if lines == 2:
        ways_across = [(cross(1) + cross(-1), tuple(jnp.where(line == 1, b, a) for b, a in zip(from_below, from_above)))]
    else:
        ways_across = [(cross(1), from_below), (cross(-1), from_above)] if lines > 1 else []
    classes = []
    for _, (near_class, far_class, valid) in ways_across:
        classes += [jnp.where(valid, near_class, -1), jnp.where(valid & relay_here, far_class, -1)]
    live_classes = [
        functools.reduce(jnp.logical_or, [found == c for found in classes], jnp.bool_(c == 0)) for c in range(CLASSES)
    ]
    meta = jnp.stack([place, left_dims[0], right_dims[0], *live_classes, *classes]).astype(jnp.int32)
    terms = functools.partial(call_terms, term_shift, meta)

    eighth = vectors // 8
    widths = [part * eighth for part in RUNS] if vectors % 8 == 0 else [vectors]
    starts = [sum(widths[:i]) for i in range(len(widths))]
    last = len(widths) - 1
    live = call_mask(meta, wavefunction, starts, widths)
    extras = ()
    if ways == 2 and SPARE:
        packed = call_pack(term_shift, meta, left_env, right_env, ways, live[-1])
        extras = [permute(part, "mpo", [(0, 1), (1, 0)]) for part in packed]
    landed, relayed, near, far, held = {}, {}, {}, {}, {}

    def send(index, tick=None):
        block = live[index]
        if tick is not None:
            block, tick = after(block, tick)
            held.setdefault((index, 0), []).append(tick)
        landed[index] = [permute(block, "sec", pairs) for pairs, _ in ways_across]

    def receive(index, tick):
        near[index], relayed[index] = [], []
        for block in landed[index]:
            block, passed = after(block, tick)
            held.setdefault((index, 0), []).append(passed)
            near[index].append(around(block))
            relayed[index].append(permute(block, "sec", relay))

    def share_far(index, tick=None):
        far[index] = []
        for part in relayed[index]:
            if tick is not None:
                part, passed = after(part, tick)
                held.setdefault((index, 1), []).append(passed)
            far[index].append(around(part))

    def add(members, total, positions, ticks):
        ticks = list(ticks)
        for way in range(len(ways_across)):
            kinds = [OWN + 2 * way + position for position in positions]
            sources = [[(far if position else near)[index][way] for index in members] for position in positions]
            waits = ticks + [t for position in positions for index in members for t in held.get((index, position), [])]
            finish = 1 in positions and way == len(ways_across) - 1
            *total, tick = terms(kinds, sources, left_env, right_env, extras, waits, total, finish=finish)
            ticks = [tick]
            if not finish:
                total = total[0]
        return total, ticks[0]

    send(0)
    *totals, tick = terms([None], [[around(wavefunction[0])]], left_env, right_env, extras, mask=True, split=widths)
    if last:
        send(1, tick)
    if ways_across:
        receive(0, tick)
        for index in range(last + 1):
            if index == last and index > 1:
                share_far(index, tick)
                totals[index], tick = add([index], totals[index], (0, 1), [tick])
                continue
            total, tick = add([index], totals[index], (0,), [tick])
            share_far(index, tick)
            if index + 1 <= last:
                receive(index + 1, tick)
            if index + 2 <= last:
                send(index + 2, tick)
            totals[index], tick = add([index], total, (1,), [tick])

    blocks = []
    for index in range(last + 1):
        sums, *gifts = totals[index] if ways_across else (totals[index][:, :share],)
        for turn, given in enumerate(gifts, 1):
            sums += permute(given, "mpo", [(i, (i + turn) % ways) for i in range(ways)]).astype(jnp.float32)
        blocks.append(jnp.where(keep_mask, sums, jnp.zeros_like(sums)).astype(jnp.bfloat16))
    return jnp.concatenate(blocks)[None]


def solution(mesh):
    in_specs = (
        P("sec", None, "mpo", None),
        P("sec", "mpo", None, None),
        P("sec", "mpo", None, None),
        P("sec"),
        P("sec"),
        P("mpo"),
    )
    out_specs = P("sec", None, "mpo", None)
    return jax.shard_map(
        per_device, mesh=mesh, in_specs=in_specs, out_specs=out_specs, check_vma=False
    )
```

time: 101 us -> 96.4 us (0.954)
  the two profiles are of different devices: /device:TPU:25 before, /device:TPU:5 now
where the time goes in v2:
time: 96.4 us; the launch traced here: 96 us
  Pallas kernels  44.6 us (46%)
  waiting for transfers between devices  28.9 us (30%)
  starting transfers between devices  12.3 us (13%)
  local copies, waits for them, and re-layouts  5.98 us (6%)
  other arithmetic  2.68 us (3%)
  between operations  1.52 us (2%)
    pallas_call x5, Pallas kernels, call_terms(): pl.pallas_call(functools.partial(sum_terms, kinds, ways, slots, len(sourc...  43.9 us
    ppermute x11, waiting for transfers between devices, permute(): lax.ppermute(array, axis, sorted(pairs))  28.9 us
    ppermute x11, starting transfers between devices, permute(): lax.ppermute(array, axis, sorted(pairs))  12.3 us
    unnamed x18, local copies, waits for them, and re-layouts  5.89 us
  transfers between devices with their start and end apart: 11, of which 4 were waited for; matrix products, arithmetic and copies ran while one was open for 0% of the time, Pallas kernels for 47%

profile of v2, /device:TPU:5, one launch (start us, length us, event | category | flops | bytes accessed | tf_op | source)
XLA Modules:
  0.0 96.0 jit_solution(3173316929081683661)
XLA Ops:
  0.0 0.7 collective-permute-start.1
  2.0 0.1 stack.47.meta_ref
  2.1 1.2 %copy-done.1 = bf16[1,8,256,256]{3,2,1,0:T(8,128)(2,1)S(1)} copy-done((bf16[1,8,256,256]{3,2,1,0:T(8,128)(2,1)S(1)}, bf16[1,8,256,256]{3,2,1,0:T(8,128)(2,1)}, u32[]{:S(2)}) %copy-start.1) | copy-done | bytes 1048600
  3.3 0.7 shard_map.64
  4.0 3.3 %collective-permute-start = (bf16[4,256,256]{2,1,0:T(8,128)(2,1)S(1)}, bf16[4,256,256]{2,1,0:T(8,128)(2,1)S(1)}, u32[]{:S(2)}, u32[]{:S(2)}) collective-permute-start(bf16[4,256,256]{2,1,0:T(8,128)(2,1)S(1)} %get-tuple-element.29), channel_id=1, source_target_pairs={{0,18},{2,16},{4,22},{6,20},{8,26},{10,24},{12,30},{14,28},{16,2},... | collective-permute-start | bytes 1572872 | tf_op jit(solution)/shard_map/ppermute | solution.py:320
  7.3 10.2 %shard_map.65 = (f32[4,512,256]{2,1,0:T(8,128)}, f32[4,512,256]{2,1,0:T(8,128)}, s32[8,128]{1,0:T(8,128)}) custom-call(s32[20]{0:T(128)} %shift_ref.9, s32[10]{0:T(128)} %copy-done.6, bf16[8,256,256]{2,1,0:T(8,128)(2,1)} %bitcast.15, bf16[8,256,256]{2,1,0:T(8,128)(2,1)} %collective-permute-done.1.refs_1_, bf16[1,20,512,512]{3,2,1,0:T(8,128)(2,1)} %refs_2_.9, ...), custom_call_target="tpu_custom_call" | custom-call | flops 1000000 | bytes 1000 | tf_op jit(solution)/shard_map/pallas_call | solution.py:278
  17.5 13.2 %collective-permute-done.refs_0_ = bf16[4,256,256]{2,1,0:T(8,128)(2,1)S(1)} collective-permute-done((bf16[4,256,256]{2,1,0:T(8,128)(2,1)S(1)}, bf16[4,256,256]{2,1,0:T(8,128)(2,1)S(1)}, u32[]{:S(2)}, u32[]{:S(2)}) %collective-permute-start) | collective-permute-done | bytes 524320 | tf_op jit(solution)/shard_map/ppermute | solution.py:320
  30.7 0.8 collective-permute-start.3
  31.5 2.3 %collective-permute-start.2 = (bf16[4,256,256]{2,1,0:T(8,128)(2,1)S(1)}, bf16[4,256,256]{2,1,0:T(8,128)(2,1)S(1)}, u32[]{:S(2)}, u32[]{:S(2)}) collective-permute-start(bf16[4,256,256]{2,1,0:T(8,128)(2,1)S(1)} %collective-permute-done.refs_0_), channel_id=1, source_target_pairs={{0,4},{4,8},{6,2},{8,12},{10,6},{14,10},{16,20},{20,24},{22,18},{2... | collective-permute-start | bytes 1572872 | tf_op jit(solution)/shard_map/ppermute | solution.py:320
  33.8 0.1 collective-permute-start.6
  33.9 0.0 copy-start
  33.9 1.7 %copy-done = bf16[1,20,256,256]{3,2,1,0:T(8,128)(2,1)S(1)} copy-done((bf16[1,20,256,256]{3,2,1,0:T(8,128)(2,1)S(1)}, bf16[1,20,256,256]{3,2,1,0:T(8,128)(2,1)}, u32[]{:S(2)}) %copy-start) | copy-done | bytes 2621464
  35.6 1.6 %copy-done.3 = f32[4,512,256]{2,1,0:T(8,128)S(1)} copy-done((f32[4,512,256]{2,1,0:T(8,128)S(1)}, f32[4,512,256]{2,1,0:T(8,128)}, u32[]{:S(2)}) %copy-start.3) | copy-done | bytes 2097176
  37.2 0.7 copy-done.4
  37.9 0.6 copy-done.7
  38.5 8.3 %shard_map.66 = (f32[4,512,256]{2,1,0:T(8,128)S(1)}, s32[8,128]{1,0:T(8,128)S(1)}) custom-call(s32[20]{0:T(128)S(1)} %copy-done.8, s32[10]{0:T(128)S(1)} %copy-done.7, bf16[4,256,256]{2,1,0:T(8,128)(2,1)S(1)} %collective-permute-done.refs_0_, bf16[4,256,256]{2,1,0:T(8,128)(2,1)S(1)} %collective-permute-done.3.refs_1_, bf16[1,20,512,512]{3,2,1,0:T(8,128)(2,1)} %refs_2_.9, ...), custom_call_target="tpu_custom_call" | custom-call | flops 1000000 | bytes 1000 | tf_op jit(solution)/shard_map/pallas_call | solution.py:278
  46.9 0.0 collective-permute-done.2.refs_0_
  46.9 0.8 collective-permute-start.4
  47.7 12.4 %collective-permute-done.6.refs_0_ = bf16[4,256,256]{2,1,0:T(8,128)(2,1)S(1)} collective-permute-done((bf16[4,256,256]{2,1,0:T(8,128)(2,1)S(1)}, bf16[4,256,256]{2,1,0:T(8,128)(2,1)S(1)}, u32[]{:S(2)}, u32[]{:S(2)}) %collective-permute-start.6) | collective-permute-done | bytes 524320 | tf_op jit(solution)/shard_map/ppermute | solution.py:320
  60.1 1.1 %collective-permute-start.8 = (bf16[4,256,256]{2,1,0:T(8,128)(2,1)S(1)}, bf16[4,256,256]{2,1,0:T(8,128)(2,1)S(1)}, u32[]{:S(2)}, u32[]{:S(2)}) collective-permute-start(bf16[4,256,256]{2,1,0:T(8,128)(2,1)S(1)} %collective-permute-done.6.refs_0_), channel_id=1, source_target_pairs={{0,1},{1,0},{2,3},{3,2},{4,5},{5,4},{6,7},{7,6},{8,9},{9,8},{10,11... | collective-permute-start | bytes 1572872 | tf_op jit(solution)/shard_map/ppermute | solution.py:320
  61.2 2.6 %collective-permute-start.7 = (bf16[4,256,256]{2,1,0:T(8,128)(2,1)S(1)}, bf16[4,256,256]{2,1,0:T(8,128)(2,1)S(1)}, u32[]{:S(2)}, u32[]{:S(2)}) collective-permute-start(bf16[4,256,256]{2,1,0:T(8,128)(2,1)S(1)} %collective-permute-done.6.refs_0_), channel_id=1, source_target_pairs={{0,4},{4,8},{6,2},{8,12},{10,6},{14,10},{16,20},{20,24},{22,18},{2... | collective-permute-start | bytes 1572872 | tf_op jit(solution)/shard_map/ppermute | solution.py:320
  63.9 8.3 %shard_map.67 = (f32[4,256,256]{2,1,0:T(8,128)S(1)}, bf16[4,256,256]{2,1,0:T(8,128)(2,1)S(1)}, s32[8,128]{1,0:T(8,128)S(1)}) custom-call(s32[20]{0:T(128)S(1)} %copy-done.8, s32[10]{0:T(128)S(1)} %copy-done.7, bf16[4,256,256]{2,1,0:T(8,128)(2,1)S(1)} %collective-permute-done.2.refs_0_, bf16[4,256,256]{2,1,0:T(8,128)(2,1)S(1)} %collective-permute-done.4.refs_1_, ...), custom_call_target="tpu_custom_call" | custom-call | flops 1000000 | bytes 1000 | tf_op jit(solution)/shard_map/pallas_call | solution.py:278
  72.2 8.3 %shard_map.68 = (f32[4,512,256]{2,1,0:T(8,128)S(1)}, s32[8,128]{1,0:T(8,128)S(1)}) custom-call(s32[20]{0:T(128)S(1)} %copy-done.8, s32[10]{0:T(128)S(1)} %copy-done.7, bf16[4,256,256]{2,1,0:T(8,128)(2,1)S(1)} %collective-permute-done.6.refs_0_, bf16[4,256,256]{2,1,0:T(8,128)(2,1)S(1)} %collective-permute-done.8.refs_1_, bf16[1,20,512,512]{3,2,1,0:T(8,128)(2,1)} %refs_2_.9, ...), custom_call_target="tpu_custom_call" | custom-call | flops 1000000 | bytes 1000 | tf_op jit(solution)/shard_map/pallas_call | solution.py:278
  80.6 0.1 collective-permute-start.9
  80.7 0.5 collective-permute-start.5
  81.2 1.4 %collective-permute-done.9.refs_1_ = bf16[4,256,256]{2,1,0:T(8,128)(2,1)S(1)} collective-permute-done((bf16[4,256,256]{2,1,0:T(8,128)(2,1)S(1)}, bf16[4,256,256]{2,1,0:T(8,128)(2,1)S(1)}, u32[]{:S(2)}, u32[]{:S(2)}) %collective-permute-start.9) | collective-permute-done | bytes 524320 | tf_op jit(solution)/shard_map/ppermute | solution.py:320
  82.6 8.8 %shard_map.69 = (f32[4,256,256]{2,1,0:T(8,128)S(1)}, bf16[4,256,256]{2,1,0:T(8,128)(2,1)S(1)}, s32[8,128]{1,0:T(8,128)}) custom-call(s32[20]{0:T(128)S(1)} %copy-done.8, s32[10]{0:T(128)S(1)} %copy-done.7, bf16[4,256,256]{2,1,0:T(8,128)(2,1)S(1)} %collective-permute-done.7.refs_0_, bf16[4,256,256]{2,1,0:T(8,128)(2,1)S(1)} %collective-permute-done.9.refs_1_, ...), custom_call_target="tpu_custom_call" | custom-call | flops 1000000 | bytes 1000 | tf_op jit(solution)/shard_map/pallas_call | solution.py:278
  91.3 0.1 collective-permute-start.10
  91.4 0.1 broadcast_and_fusion
  91.6 1.9 %collective-permute-done.10 = bf16[4,256,256]{2,1,0:T(8,128)(2,1)} collective-permute-done((bf16[4,256,256]{2,1,0:T(8,128)(2,1)S(1)}, bf16[4,256,256]{2,1,0:T(8,128)(2,1)}, u32[]{:S(2)}, u32[]{:S(2)}) %collective-permute-start.10) | collective-permute-done | bytes 524320 | tf_op jit(solution)/shard_map/ppermute | solution.py:320
  93.5 1.5 %select_convert_fusion.1 = (bf16[4,256,256]{2,1,0:T(8,128)(2,1)S(1)}, bf16[4,256,256]{2,1,0:T(8,128)(2,1)S(1)}) fusion(f32[4,256,256]{2,1,0:T(8,128)S(1)} %get-tuple-element.38, bf16[4,256,256]{2,1,0:T(8,128)(2,1)} %collective-permute-done.5, pred[256,256]{1,0:T(8,128)(4,1)S(1)} %broadcast_and_fusion, f32[4,256,256]{2,1,0:T(8,128)S(1)} %get-tuple-element.51, ...), kind=kLoop, calls=%fused_computation.2 | loop fusion | flops 2097152 | bytes 4259840 | tf_op jit(solution)/shard_map/convert_element_type | solution.py:447
  95.0 1.1 %maximum_bitcast_fusion = bf16[1,8,256,256]{3,2,1,0:T(8,128)(2,1)} fusion(bf16[4,256,256]{2,1,0:T(8,128)(2,1)S(1)} %get-tuple-element.54, bf16[4,256,256]{2,1,0:T(8,128)(2,1)S(1)} %get-tuple-element.53), kind=kLoop, calls=%fused_computation | loop fusion | flops 524288 | bytes 2097152 | tf_op jit(solution)/shard_map/broadcast_in_dim | solution.py:448
  (19 shorter events, 0.1 us)
Async XLA Ops:
  0.0 7.3 %collective-permute-start.1 = (bf16[8,256,256]{2,1,0:T(8,128)(2,1)}, bf16[8,256,256]{2,1,0:T(8,128)(2,1)}, u32[]{:S(2)}, u32[]{:S(2)}) collective-permute-start(bf16[8,256,256]{2,1,0:T(8,128)(2,1)} %bitcast.14), channel_id=1, source_target_pairs={{0,1},{1,0},{2,3},{3,2},{4,5},{5,4},{6,7},{7,6},{8,9},{9,8},{10,11... | collective-permute-start | bytes 3145736 | tf_op jit(solution)/shard_map/ppermute | solution.py:320
  2.1 1.2 %copy-start.1 = (bf16[1,8,256,256]{3,2,1,0:T(8,128)(2,1)S(1)}, bf16[1,8,256,256]{3,2,1,0:T(8,128)(2,1)}, u32[]{:S(2)}) copy-start(bf16[1,8,256,256]{3,2,1,0:T(8,128)(2,1)} %source_ref.1) | copy-start | bytes 3145732
  3.3 4.1 %copy-start.6 = (s32[10]{0:T(128)}, s32[10]{0:T(128)S(1)}, u32[]{:S(2)}) copy-start(s32[10]{0:T(128)S(1)} %stack.47.meta_ref) | copy-start | bytes 124
  4.0 29.8 %copy-start.8 = (s32[20]{0:T(128)S(1)}, s32[20]{0:T(128)}, u32[]{:S(2)}) copy-start(s32[20]{0:T(128)} %shift_ref.9) | copy-start | bytes 244
  4.0 26.7 %collective-permute-start = (bf16[4,256,256]{2,1,0:T(8,128)(2,1)S(1)}, bf16[4,256,256]{2,1,0:T(8,128)(2,1)S(1)}, u32[]{:S(2)}, u32[]{:S(2)}) collective-permute-start(bf16[4,256,256]{2,1,0:T(8,128)(2,1)S(1)} %get-tuple-element.29), channel_id=1, source_target_pairs={{0,18},{2,16},{4,22},{6,20},{8,26},{10,24},{12,30},{14,28},{16,2},... | collective-permute-start | bytes 1572872 | tf_op jit(solution)/shard_map/ppermute | solution.py:320
  30.7 3.2 %collective-permute-start.3 = (bf16[4,256,256]{2,1,0:T(8,128)(2,1)S(1)}, bf16[4,256,256]{2,1,0:T(8,128)(2,1)S(1)}, u32[]{:S(2)}, u32[]{:S(2)}) collective-permute-start(bf16[4,256,256]{2,1,0:T(8,128)(2,1)S(1)} %collective-permute-done.refs_0_), channel_id=1, source_target_pairs={{0,1},{1,0},{2,3},{3,2},{4,5},{5,4},{6,7},{7,6},{8,9},{9,8},{10,11... | collective-permute-start | bytes 1572872 | tf_op jit(solution)/shard_map/ppermute | solution.py:320
  31.5 15.4 %collective-permute-start.2 = (bf16[4,256,256]{2,1,0:T(8,128)(2,1)S(1)}, bf16[4,256,256]{2,1,0:T(8,128)(2,1)S(1)}, u32[]{:S(2)}, u32[]{:S(2)}) collective-permute-start(bf16[4,256,256]{2,1,0:T(8,128)(2,1)S(1)} %collective-permute-done.refs_0_), channel_id=1, source_target_pairs={{0,4},{4,8},{6,2},{8,12},{10,6},{14,10},{16,20},{20,24},{22,18},{2... | collective-permute-start | bytes 1572872 | tf_op jit(solution)/shard_map/ppermute | solution.py:320
  33.8 26.3 %collective-permute-start.6 = (bf16[4,256,256]{2,1,0:T(8,128)(2,1)S(1)}, bf16[4,256,256]{2,1,0:T(8,128)(2,1)S(1)}, u32[]{:S(2)}, u32[]{:S(2)}) collective-permute-start(bf16[4,256,256]{2,1,0:T(8,128)(2,1)S(1)} %get-tuple-element.41), channel_id=1, source_target_pairs={{0,18},{2,16},{4,22},{6,20},{8,26},{10,24},{12,30},{14,28},{16,2},... | collective-permute-start | bytes 1572872 | tf_op jit(solution)/shard_map/ppermute | solution.py:320
  33.9 1.7 %copy-start = (bf16[1,20,256,256]{3,2,1,0:T(8,128)(2,1)S(1)}, bf16[1,20,256,256]{3,2,1,0:T(8,128)(2,1)}, u32[]{:S(2)}) copy-start(bf16[1,20,256,256]{3,2,1,0:T(8,128)(2,1)} %refs_3_.9) | copy-start | bytes 7864324
  35.6 1.6 %copy-start.3 = (f32[4,512,256]{2,1,0:T(8,128)S(1)}, f32[4,512,256]{2,1,0:T(8,128)}, u32[]{:S(2)}) copy-start(f32[4,512,256]{2,1,0:T(8,128)} %get-tuple-element.33.refs_6_) | copy-start | bytes 6291460
  37.2 0.7 copy-start.4
  37.9 0.6 copy-start.7
  46.9 16.9 %collective-permute-start.4 = (bf16[4,256,256]{2,1,0:T(8,128)(2,1)S(1)}, bf16[4,256,256]{2,1,0:T(8,128)(2,1)S(1)}, u32[]{:S(2)}, u32[]{:S(2)}) collective-permute-start(bf16[4,256,256]{2,1,0:T(8,128)(2,1)S(1)} %collective-permute-done.2.refs_0_), channel_id=1, source_target_pairs={{0,1},{1,0},{2,3},{3,2},{4,5},{5,4},{6,7},{7,6},{8,9},{9,8},{10,11... | collective-permute-start | bytes 1572872 | tf_op jit(solution)/shard_map/ppermute | solution.py:320
  60.1 12.1 %collective-permute-start.8 = (bf16[4,256,256]{2,1,0:T(8,128)(2,1)S(1)}, bf16[4,256,256]{2,1,0:T(8,128)(2,1)S(1)}, u32[]{:S(2)}, u32[]{:S(2)}) collective-permute-start(bf16[4,256,256]{2,1,0:T(8,128)(2,1)S(1)} %collective-permute-done.6.refs_0_), channel_id=1, source_target_pairs={{0,1},{1,0},{2,3},{3,2},{4,5},{5,4},{6,7},{7,6},{8,9},{9,8},{10,11... | collective-permute-start | bytes 1572872 | tf_op jit(solution)/shard_map/ppermute | solution.py:320
  61.2 19.4 %collective-permute-start.7 = (bf16[4,256,256]{2,1,0:T(8,128)(2,1)S(1)}, bf16[4,256,256]{2,1,0:T(8,128)(2,1)S(1)}, u32[]{:S(2)}, u32[]{:S(2)}) collective-permute-start(bf16[4,256,256]{2,1,0:T(8,128)(2,1)S(1)} %collective-permute-done.6.refs_0_), channel_id=1, source_target_pairs={{0,4},{4,8},{6,2},{8,12},{10,6},{14,10},{16,20},{20,24},{22,18},{2... | collective-permute-start | bytes 1572872 | tf_op jit(solution)/shard_map/ppermute | solution.py:320
  63.9 8.3 %copy-start.2 = (f32[4,512,256]{2,1,0:T(8,128)S(1)}, f32[4,512,256]{2,1,0:T(8,128)}, u32[]{:S(2)}) copy-start(f32[4,512,256]{2,1,0:T(8,128)} %get-tuple-element.46.refs_7_) | copy-start | bytes 6291460
  63.9 8.3 %copy-start.5 = (s32[8,128]{1,0:T(8,128)S(1)}, s32[8,128]{1,0:T(8,128)}, u32[]{:S(2)}) copy-start(s32[8,128]{1,0:T(8,128)} %get-tuple-element.44.refs_4_.refs_5_) | copy-start | bytes 12292
  80.6 2.0 %collective-permute-start.9 = (bf16[4,256,256]{2,1,0:T(8,128)(2,1)S(1)}, bf16[4,256,256]{2,1,0:T(8,128)(2,1)S(1)}, u32[]{:S(2)}, u32[]{:S(2)}) collective-permute-start(bf16[4,256,256]{2,1,0:T(8,128)(2,1)S(1)} %collective-permute-done.7.refs_0_), channel_id=1, source_target_pairs={{0,1},{1,0},{2,3},{3,2},{4,5},{5,4},{6,7},{7,6},{8,9},{9,8},{10,11... | collective-permute-start | bytes 1572872 | tf_op jit(solution)/shard_map/ppermute | solution.py:320
  80.7 10.9 %collective-permute-start.5 = (bf16[4,256,256]{2,1,0:T(8,128)(2,1)S(1)}, bf16[4,256,256]{2,1,0:T(8,128)(2,1)}, u32[]{:S(2)}, u32[]{:S(2)}) collective-permute-start(bf16[4,256,256]{2,1,0:T(8,128)(2,1)S(1)} %get-tuple-element.39), channel_id=1, source_target_pairs={{0,1},{1,0},{2,3},{3,2},{4,5},{5,4},{6,7},{7,6},{8,9},{9,8},{10,11... | collective-permute-start | bytes 1572872 | tf_op jit(solution)/shard_map/ppermute | solution.py:320
  91.3 2.1 %collective-permute-start.10 = (bf16[4,256,256]{2,1,0:T(8,128)(2,1)S(1)}, bf16[4,256,256]{2,1,0:T(8,128)(2,1)}, u32[]{:S(2)}, u32[]{:S(2)}) collective-permute-start(bf16[4,256,256]{2,1,0:T(8,128)(2,1)S(1)} %get-tuple-element.52), channel_id=1, source_target_pairs={{0,1},{1,0},{2,3},{3,2},{4,5},{5,4},{6,7},{7,6},{8,9},{9,8},{10,11... | collective-permute-start | bytes 1572872 | tf_op jit(solution)/shard_map/ppermute | solution.py:320

commit v3 on v2

--- a/solution.py
+++ b/solution.py
@@ -12,7 +12,7 @@
 SPARE = 0
 VMEM = 40 * 2**20
 WHOLE_VMEM = 62 * 2**20
-RUNS = (4, 4)
+RUNS = (3, 5)
 PLACE, LEFT, RIGHT, LIVE, OWN = 0, 1, 2, 3, 3 + CLASSES
 HINT = pl.CostEstimate(flops=10**6, bytes_accessed=10**3, transcendentals=0)
 

time: 96.4 us -> 94.2 us (0.977)
  the two profiles are of different devices: /device:TPU:5 before, /device:TPU:25 now
where the time goes in v3:
time: 94.2 us; the launch traced here: 94.5 us
  Pallas kernels  39.2 us (42%)
  waiting for transfers between devices  31 us (33%)
  starting transfers between devices  14.5 us (15%)
  local copies, waits for them, and re-layouts  5.77 us (6%)
  other arithmetic  2.61 us (3%)
  between operations  1.47 us (2%)
    pallas_call x5, Pallas kernels, call_terms(): pl.pallas_call(functools.partial(sum_terms, kinds, ways, slots, len(sourc...  38.4 us
    ppermute x11, waiting for transfers between devices, permute(): lax.ppermute(array, axis, sorted(pairs))  31 us
    ppermute x11, starting transfers between devices, permute(): lax.ppermute(array, axis, sorted(pairs))  14.5 us
    unnamed x18, local copies, waits for them, and re-layouts  5.68 us
  transfers between devices with their start and end apart: 11, of which 7 were waited for; matrix products, arithmetic and copies ran while one was open for 0% of the time, Pallas kernels for 41%

profile of v3, /device:TPU:25, one launch (start us, length us, event | category | flops | bytes accessed | tf_op | source)
XLA Modules:
  0.0 94.5 jit_solution(4430891083358512074)
XLA Ops:
  0.0 0.7 collective-permute-start.1
  2.0 0.1 stack.47.meta_ref
  2.1 1.2 %copy-done.1 = bf16[1,8,256,256]{3,2,1,0:T(8,128)(2,1)S(1)} copy-done((bf16[1,8,256,256]{3,2,1,0:T(8,128)(2,1)S(1)}, bf16[1,8,256,256]{3,2,1,0:T(8,128)(2,1)}, u32[]{:S(2)}) %copy-start.1) | copy-done | bytes 1048600
  3.3 0.7 shard_map.64
  4.0 1.0 %collective-permute-start = (bf16[3,256,256]{2,1,0:T(8,128)(2,1)S(1)}, bf16[3,256,256]{2,1,0:T(8,128)(2,1)S(1)}, u32[]{:S(2)}, u32[]{:S(2)}) collective-permute-start(bf16[3,256,256]{2,1,0:T(8,128)(2,1)S(1)} %get-tuple-element.29), channel_id=1, source_target_pairs={{0,18},{2,16},{4,22},{6,20},{8,26},{10,24},{12,30},{14,28},{16,2},... | collective-permute-start | bytes 1179656 | tf_op jit(solution)/shard_map/ppermute | solution.py:320
  5.1 15.6 %shard_map.65 = (f32[3,512,256]{2,1,0:T(8,128)}, f32[5,512,256]{2,1,0:T(8,128)}, s32[8,128]{1,0:T(8,128)}) custom-call(s32[20]{0:T(128)} %shift_ref.9, s32[10]{0:T(128)} %copy-done.6, bf16[8,256,256]{2,1,0:T(8,128)(2,1)} %bitcast.15, bf16[8,256,256]{2,1,0:T(8,128)(2,1)} %collective-permute-done.1.refs_1_, bf16[1,20,512,512]{3,2,1,0:T(8,128)(2,1)} %refs_2_.9, ...), custom_call_target="tpu_custom_call" | custom-call | flops 1000000 | bytes 1000 | tf_op jit(solution)/shard_map/pallas_call | solution.py:278
  20.7 2.3 %collective-permute-start.6 = (bf16[5,256,256]{2,1,0:T(8,128)(2,1)S(1)}, bf16[5,256,256]{2,1,0:T(8,128)(2,1)S(1)}, u32[]{:S(2)}, u32[]{:S(2)}) collective-permute-start(bf16[5,256,256]{2,1,0:T(8,128)(2,1)S(1)} %get-tuple-element.41), channel_id=1, source_target_pairs={{0,18},{2,16},{4,22},{6,20},{8,26},{10,24},{12,30},{14,28},{16,2},... | collective-permute-start | bytes 1966088 | tf_op jit(solution)/shard_map/ppermute | solution.py:320
  23.1 16.3 %collective-permute-done.refs_0_ = bf16[3,256,256]{2,1,0:T(8,128)(2,1)S(1)} collective-permute-done((bf16[3,256,256]{2,1,0:T(8,128)(2,1)S(1)}, bf16[3,256,256]{2,1,0:T(8,128)(2,1)S(1)}, u32[]{:S(2)}, u32[]{:S(2)}) %collective-permute-start) | collective-permute-done | bytes 393248 | tf_op jit(solution)/shard_map/ppermute | solution.py:320
  39.3 0.5 collective-permute-start.3
  39.8 3.1 %collective-permute-start.2 = (bf16[3,256,256]{2,1,0:T(8,128)(2,1)S(1)}, bf16[3,256,256]{2,1,0:T(8,128)(2,1)S(1)}, u32[]{:S(2)}, u32[]{:S(2)}) collective-permute-start(bf16[3,256,256]{2,1,0:T(8,128)(2,1)S(1)} %collective-permute-done.refs_0_), channel_id=1, source_target_pairs={{0,4},{4,8},{6,2},{8,12},{10,6},{14,10},{16,20},{20,24},{22,18},{2... | collective-permute-start | bytes 1179656 | tf_op jit(solution)/shard_map/ppermute | solution.py:320
  43.0 1.7 %copy-done = bf16[1,20,256,256]{3,2,1,0:T(8,128)(2,1)S(1)} copy-done((bf16[1,20,256,256]{3,2,1,0:T(8,128)(2,1)S(1)}, bf16[1,20,256,256]{3,2,1,0:T(8,128)(2,1)}, u32[]{:S(2)}) %copy-start) | copy-done | bytes 2621464
  44.7 1.4 %copy-done.3 = f32[3,512,256]{2,1,0:T(8,128)S(1)} copy-done((f32[3,512,256]{2,1,0:T(8,128)S(1)}, f32[3,512,256]{2,1,0:T(8,128)}, u32[]{:S(2)}) %copy-start.3) | copy-done | bytes 1572888
  46.1 0.7 copy-done.4
  46.8 0.6 copy-done.7
  47.4 3.7 %shard_map.66 = (f32[3,512,256]{2,1,0:T(8,128)S(1)}, s32[8,128]{1,0:T(8,128)S(1)}) custom-call(s32[20]{0:T(128)S(1)} %copy-done.8, s32[10]{0:T(128)S(1)} %copy-done.7, bf16[3,256,256]{2,1,0:T(8,128)(2,1)S(1)} %collective-permute-done.refs_0_, bf16[3,256,256]{2,1,0:T(8,128)(2,1)S(1)} %collective-permute-done.3.refs_1_, bf16[1,20,512,512]{3,2,1,0:T(8,128)(2,1)} %refs_2_.9, ...), custom_call_target="tpu_custom_call" | custom-call | flops 1000000 | bytes 1000 | tf_op jit(solution)/shard_map/pallas_call | solution.py:278
  51.2 2.2 %collective-permute-done.6.refs_0_ = bf16[5,256,256]{2,1,0:T(8,128)(2,1)S(1)} collective-permute-done((bf16[5,256,256]{2,1,0:T(8,128)(2,1)S(1)}, bf16[5,256,256]{2,1,0:T(8,128)(2,1)S(1)}, u32[]{:S(2)}, u32[]{:S(2)}) %collective-permute-start.6) | collective-permute-done | bytes 655392 | tf_op jit(solution)/shard_map/ppermute | solution.py:320
  53.4 0.9 collective-permute-start.8
  54.3 2.7 %collective-permute-start.7 = (bf16[5,256,256]{2,1,0:T(8,128)(2,1)S(1)}, bf16[5,256,256]{2,1,0:T(8,128)(2,1)S(1)}, u32[]{:S(2)}, u32[]{:S(2)}) collective-permute-start(bf16[5,256,256]{2,1,0:T(8,128)(2,1)S(1)} %collective-permute-done.6.refs_0_), channel_id=1, source_target_pairs={{0,4},{4,8},{6,2},{8,12},{10,6},{14,10},{16,20},{20,24},{22,18},{2... | collective-permute-start | bytes 1966088 | tf_op jit(solution)/shard_map/ppermute | solution.py:320
  57.0 5.8 %collective-permute-done.2.refs_0_ = bf16[3,256,256]{2,1,0:T(8,128)(2,1)S(1)} collective-permute-done((bf16[3,256,256]{2,1,0:T(8,128)(2,1)S(1)}, bf16[3,256,256]{2,1,0:T(8,128)(2,1)S(1)}, u32[]{:S(2)}, u32[]{:S(2)}) %collective-permute-start.2) | collective-permute-done | bytes 393248 | tf_op jit(solution)/shard_map/ppermute | solution.py:320
  62.8 0.5 collective-permute-start.4
  63.3 1.3 %collective-permute-done.4.refs_1_ = bf16[3,256,256]{2,1,0:T(8,128)(2,1)S(1)} collective-permute-done((bf16[3,256,256]{2,1,0:T(8,128)(2,1)S(1)}, bf16[3,256,256]{2,1,0:T(8,128)(2,1)S(1)}, u32[]{:S(2)}, u32[]{:S(2)}) %collective-permute-start.4) | collective-permute-done | bytes 393248 | tf_op jit(solution)/shard_map/ppermute | solution.py:320
  64.6 6.0 %shard_map.67 = (f32[3,256,256]{2,1,0:T(8,128)S(1)}, bf16[3,256,256]{2,1,0:T(8,128)(2,1)S(1)}, s32[8,128]{1,0:T(8,128)S(1)}) custom-call(s32[20]{0:T(128)S(1)} %copy-done.8, s32[10]{0:T(128)S(1)} %copy-done.7, bf16[3,256,256]{2,1,0:T(8,128)(2,1)S(1)} %collective-permute-done.2.refs_0_, bf16[3,256,256]{2,1,0:T(8,128)(2,1)S(1)} %collective-permute-done.4.refs_1_, ...), custom_call_target="tpu_custom_call" | custom-call | flops 1000000 | bytes 1000 | tf_op jit(solution)/shard_map/pallas_call | solution.py:278
  70.7 4.3 %shard_map.68 = (f32[5,512,256]{2,1,0:T(8,128)S(1)}, s32[8,128]{1,0:T(8,128)S(1)}) custom-call(s32[20]{0:T(128)S(1)} %copy-done.8, s32[10]{0:T(128)S(1)} %copy-done.7, bf16[5,256,256]{2,1,0:T(8,128)(2,1)S(1)} %collective-permute-done.6.refs_0_, bf16[5,256,256]{2,1,0:T(8,128)(2,1)S(1)} %collective-permute-done.8.refs_1_, bf16[1,20,512,512]{3,2,1,0:T(8,128)(2,1)} %refs_2_.9, ...), custom_call_target="tpu_custom_call" | custom-call | flops 1000000 | bytes 1000 | tf_op jit(solution)/shard_map/pallas_call | solution.py:278
  75.1 1.8 %collective-permute-done.7.refs_0_ = bf16[5,256,256]{2,1,0:T(8,128)(2,1)S(1)} collective-permute-done((bf16[5,256,256]{2,1,0:T(8,128)(2,1)S(1)}, bf16[5,256,256]{2,1,0:T(8,128)(2,1)S(1)}, u32[]{:S(2)}, u32[]{:S(2)}) %collective-permute-start.7) | collective-permute-done | bytes 655392 | tf_op jit(solution)/shard_map/ppermute | solution.py:320
  76.8 2.6 %collective-permute-start.9 = (bf16[5,256,256]{2,1,0:T(8,128)(2,1)S(1)}, bf16[5,256,256]{2,1,0:T(8,128)(2,1)S(1)}, u32[]{:S(2)}, u32[]{:S(2)}) collective-permute-start(bf16[5,256,256]{2,1,0:T(8,128)(2,1)S(1)} %collective-permute-done.7.refs_0_), channel_id=1, source_target_pairs={{0,1},{1,0},{2,3},{3,2},{4,5},{5,4},{6,7},{7,6},{8,9},{9,8},{10,11... | collective-permute-start | bytes 1966088 | tf_op jit(solution)/shard_map/ppermute | solution.py:320
  79.5 1.6 %collective-permute-done.9.refs_1_ = bf16[5,256,256]{2,1,0:T(8,128)(2,1)S(1)} collective-permute-done((bf16[5,256,256]{2,1,0:T(8,128)(2,1)S(1)}, bf16[5,256,256]{2,1,0:T(8,128)(2,1)S(1)}, u32[]{:S(2)}, u32[]{:S(2)}) %collective-permute-start.9) | collective-permute-done | bytes 655392 | tf_op jit(solution)/shard_map/ppermute | solution.py:320
  81.2 8.7 %shard_map.69 = (f32[5,256,256]{2,1,0:T(8,128)S(1)}, bf16[5,256,256]{2,1,0:T(8,128)(2,1)S(1)}, s32[8,128]{1,0:T(8,128)}) custom-call(s32[20]{0:T(128)S(1)} %copy-done.8, s32[10]{0:T(128)S(1)} %copy-done.7, bf16[5,256,256]{2,1,0:T(8,128)(2,1)S(1)} %collective-permute-done.7.refs_0_, bf16[5,256,256]{2,1,0:T(8,128)(2,1)S(1)} %collective-permute-done.9.refs_1_, ...), custom_call_target="tpu_custom_call" | custom-call | flops 1000000 | bytes 1000 | tf_op jit(solution)/shard_map/pallas_call | solution.py:278
  90.0 0.1 broadcast_and_fusion
  90.1 0.2 select_convert_fusion.1
  90.3 1.9 %collective-permute-done.10 = bf16[5,256,256]{2,1,0:T(8,128)(2,1)} collective-permute-done((bf16[5,256,256]{2,1,0:T(8,128)(2,1)S(1)}, bf16[5,256,256]{2,1,0:T(8,128)(2,1)}, u32[]{:S(2)}, u32[]{:S(2)}) %collective-permute-start.10) | collective-permute-done | bytes 655392 | tf_op jit(solution)/shard_map/ppermute | solution.py:320
  92.2 1.3 %select_convert_fusion = bf16[5,256,256]{2,1,0:T(8,128)(2,1)S(1)} fusion(f32[5,256,256]{2,1,0:T(8,128)S(1)} %get-tuple-element.51, bf16[5,256,256]{2,1,0:T(8,128)(2,1)} %collective-permute-done.10, pred[256,256]{1,0:T(8,128)(4,1)S(1)} %broadcast_and_fusion), kind=kLoop, calls=%fused_computation | loop fusion | flops 1310720 | bytes 2686976 | tf_op jit(solution)/shard_map/convert_element_type | solution.py:447
  93.5 1.1 %maximum_bitcast_fusion = bf16[1,8,256,256]{3,2,1,0:T(8,128)(2,1)} fusion(bf16[5,256,256]{2,1,0:T(8,128)(2,1)S(1)} %select_convert_fusion, bf16[3,256,256]{2,1,0:T(8,128)(2,1)S(1)} %select_convert_fusion.1), kind=kLoop, calls=%fused_computation.1 | loop fusion | flops 524288 | bytes 2097152 | tf_op jit(solution)/shard_map/broadcast_in_dim | solution.py:448
  (20 shorter events, 0.2 us)
Async XLA Ops:
  0.0 5.1 %collective-permute-start.1 = (bf16[8,256,256]{2,1,0:T(8,128)(2,1)}, bf16[8,256,256]{2,1,0:T(8,128)(2,1)}, u32[]{:S(2)}, u32[]{:S(2)}) collective-permute-start(bf16[8,256,256]{2,1,0:T(8,128)(2,1)} %bitcast.14), channel_id=1, source_target_pairs={{0,1},{1,0},{2,3},{3,2},{4,5},{5,4},{6,7},{7,6},{8,9},{9,8},{10,11... | collective-permute-start | bytes 3145736 | tf_op jit(solution)/shard_map/ppermute | solution.py:320
  2.1 1.2 %copy-start.1 = (bf16[1,8,256,256]{3,2,1,0:T(8,128)(2,1)S(1)}, bf16[1,8,256,256]{3,2,1,0:T(8,128)(2,1)}, u32[]{:S(2)}) copy-start(bf16[1,8,256,256]{3,2,1,0:T(8,128)(2,1)} %source_ref.1) | copy-start | bytes 3145732
  3.3 1.8 %copy-start.6 = (s32[10]{0:T(128)}, s32[10]{0:T(128)S(1)}, u32[]{:S(2)}) copy-start(s32[10]{0:T(128)S(1)} %stack.47.meta_ref) | copy-start | bytes 124
  4.0 39.0 %copy-start.8 = (s32[20]{0:T(128)S(1)}, s32[20]{0:T(128)}, u32[]{:S(2)}) copy-start(s32[20]{0:T(128)} %shift_ref.9) | copy-start | bytes 244
  4.0 35.3 %collective-permute-start = (bf16[3,256,256]{2,1,0:T(8,128)(2,1)S(1)}, bf16[3,256,256]{2,1,0:T(8,128)(2,1)S(1)}, u32[]{:S(2)}, u32[]{:S(2)}) collective-permute-start(bf16[3,256,256]{2,1,0:T(8,128)(2,1)S(1)} %get-tuple-element.29), channel_id=1, source_target_pairs={{0,18},{2,16},{4,22},{6,20},{8,26},{10,24},{12,30},{14,28},{16,2},... | collective-permute-start | bytes 1179656 | tf_op jit(solution)/shard_map/ppermute | solution.py:320
  20.7 32.7 %collective-permute-start.6 = (bf16[5,256,256]{2,1,0:T(8,128)(2,1)S(1)}, bf16[5,256,256]{2,1,0:T(8,128)(2,1)S(1)}, u32[]{:S(2)}, u32[]{:S(2)}) collective-permute-start(bf16[5,256,256]{2,1,0:T(8,128)(2,1)S(1)} %get-tuple-element.41), channel_id=1, source_target_pairs={{0,18},{2,16},{4,22},{6,20},{8,26},{10,24},{12,30},{14,28},{16,2},... | collective-permute-start | bytes 1966088 | tf_op jit(solution)/shard_map/ppermute | solution.py:320
  39.3 3.6 %collective-permute-start.3 = (bf16[3,256,256]{2,1,0:T(8,128)(2,1)S(1)}, bf16[3,256,256]{2,1,0:T(8,128)(2,1)S(1)}, u32[]{:S(2)}, u32[]{:S(2)}) collective-permute-start(bf16[3,256,256]{2,1,0:T(8,128)(2,1)S(1)} %collective-permute-done.refs_0_), channel_id=1, source_target_pairs={{0,1},{1,0},{2,3},{3,2},{4,5},{5,4},{6,7},{7,6},{8,9},{9,8},{10,11... | collective-permute-start | bytes 1179656 | tf_op jit(solution)/shard_map/ppermute | solution.py:320
  39.8 23.0 %collective-permute-start.2 = (bf16[3,256,256]{2,1,0:T(8,128)(2,1)S(1)}, bf16[3,256,256]{2,1,0:T(8,128)(2,1)S(1)}, u32[]{:S(2)}, u32[]{:S(2)}) collective-permute-start(bf16[3,256,256]{2,1,0:T(8,128)(2,1)S(1)} %collective-permute-done.refs_0_), channel_id=1, source_target_pairs={{0,4},{4,8},{6,2},{8,12},{10,6},{14,10},{16,20},{20,24},{22,18},{2... | collective-permute-start | bytes 1179656 | tf_op jit(solution)/shard_map/ppermute | solution.py:320
  43.0 1.7 %copy-start = (bf16[1,20,256,256]{3,2,1,0:T(8,128)(2,1)S(1)}, bf16[1,20,256,256]{3,2,1,0:T(8,128)(2,1)}, u32[]{:S(2)}) copy-start(bf16[1,20,256,256]{3,2,1,0:T(8,128)(2,1)} %refs_3_.9) | copy-start | bytes 7864324
  44.7 1.4 %copy-start.3 = (f32[3,512,256]{2,1,0:T(8,128)S(1)}, f32[3,512,256]{2,1,0:T(8,128)}, u32[]{:S(2)}) copy-start(f32[3,512,256]{2,1,0:T(8,128)} %get-tuple-element.33.refs_6_) | copy-start | bytes 4718596
  46.1 0.7 copy-start.4
  46.8 0.6 copy-start.7
  53.4 17.3 %collective-permute-start.8 = (bf16[5,256,256]{2,1,0:T(8,128)(2,1)S(1)}, bf16[5,256,256]{2,1,0:T(8,128)(2,1)S(1)}, u32[]{:S(2)}, u32[]{:S(2)}) collective-permute-start(bf16[5,256,256]{2,1,0:T(8,128)(2,1)S(1)} %collective-permute-done.6.refs_0_), channel_id=1, source_target_pairs={{0,1},{1,0},{2,3},{3,2},{4,5},{5,4},{6,7},{7,6},{8,9},{9,8},{10,11... | collective-permute-start | bytes 1966088 | tf_op jit(solution)/shard_map/ppermute | solution.py:320
  54.3 22.5 %collective-permute-start.7 = (bf16[5,256,256]{2,1,0:T(8,128)(2,1)S(1)}, bf16[5,256,256]{2,1,0:T(8,128)(2,1)S(1)}, u32[]{:S(2)}, u32[]{:S(2)}) collective-permute-start(bf16[5,256,256]{2,1,0:T(8,128)(2,1)S(1)} %collective-permute-done.6.refs_0_), channel_id=1, source_target_pairs={{0,4},{4,8},{6,2},{8,12},{10,6},{14,10},{16,20},{20,24},{22,18},{2... | collective-permute-start | bytes 1966088 | tf_op jit(solution)/shard_map/ppermute | solution.py:320
  62.8 1.8 %collective-permute-start.4 = (bf16[3,256,256]{2,1,0:T(8,128)(2,1)S(1)}, bf16[3,256,256]{2,1,0:T(8,128)(2,1)S(1)}, u32[]{:S(2)}, u32[]{:S(2)}) collective-permute-start(bf16[3,256,256]{2,1,0:T(8,128)(2,1)S(1)} %collective-permute-done.2.refs_0_), channel_id=1, source_target_pairs={{0,1},{1,0},{2,3},{3,2},{4,5},{5,4},{6,7},{7,6},{8,9},{9,8},{10,11... | collective-permute-start | bytes 1179656 | tf_op jit(solution)/shard_map/ppermute | solution.py:320
  64.6 6.1 %copy-start.2 = (f32[5,512,256]{2,1,0:T(8,128)S(1)}, f32[5,512,256]{2,1,0:T(8,128)}, u32[]{:S(2)}) copy-start(f32[5,512,256]{2,1,0:T(8,128)} %get-tuple-element.46.refs_7_) | copy-start | bytes 7864324
  64.6 6.1 %copy-start.5 = (s32[8,128]{1,0:T(8,128)S(1)}, s32[8,128]{1,0:T(8,128)}, u32[]{:S(2)}) copy-start(s32[8,128]{1,0:T(8,128)} %get-tuple-element.44.refs_4_.refs_5_) | copy-start | bytes 12292
  76.8 4.3 %collective-permute-start.9 = (bf16[5,256,256]{2,1,0:T(8,128)(2,1)S(1)}, bf16[5,256,256]{2,1,0:T(8,128)(2,1)S(1)}, u32[]{:S(2)}, u32[]{:S(2)}) collective-permute-start(bf16[5,256,256]{2,1,0:T(8,128)(2,1)S(1)} %collective-permute-done.7.refs_0_), channel_id=1, source_target_pairs={{0,1},{1,0},{2,3},{3,2},{4,5},{5,4},{6,7},{7,6},{8,9},{9,8},{10,11... | collective-permute-start | bytes 1966088 | tf_op jit(solution)/shard_map/ppermute | solution.py:320
  79.5 10.6 %collective-permute-start.5 = (bf16[3,256,256]{2,1,0:T(8,128)(2,1)S(1)}, bf16[3,256,256]{2,1,0:T(8,128)(2,1)S(1)}, u32[]{:S(2)}, u32[]{:S(2)}) collective-permute-start(bf16[3,256,256]{2,1,0:T(8,128)(2,1)S(1)} %get-tuple-element.39), channel_id=1, source_target_pairs={{0,1},{1,0},{2,3},{3,2},{4,5},{5,4},{6,7},{7,6},{8,9},{9,8},{10,11... | collective-permute-start | bytes 1179656 | tf_op jit(solution)/shard_map/ppermute | solution.py:320
  89.9 2.3 %collective-permute-start.10 = (bf16[5,256,256]{2,1,0:T(8,128)(2,1)S(1)}, bf16[5,256,256]{2,1,0:T(8,128)(2,1)}, u32[]{:S(2)}, u32[]{:S(2)}) collective-permute-start(bf16[5,256,256]{2,1,0:T(8,128)(2,1)S(1)} %get-tuple-element.52), channel_id=1, source_target_pairs={{0,1},{1,0},{2,3},{3,2},{4,5},{5,4},{6,7},{7,6},{8,9},{9,8},{10,11... | collective-permute-start | bytes 1966088 | tf_op jit(solution)/shard_map/ppermute | solution.py:320

commit v4 on v3

--- a/solution.py
+++ b/solution.py
@@ -12,7 +12,7 @@
 SPARE = 0
 VMEM = 40 * 2**20
 WHOLE_VMEM = 62 * 2**20
-RUNS = (3, 5)
+RUNS = (3, 3, 2)
 PLACE, LEFT, RIGHT, LIVE, OWN = 0, 1, 2, 3, 3 + CLASSES
 HINT = pl.CostEstimate(flops=10**6, bytes_accessed=10**3, transcendentals=0)
 
@@ -377,6 +377,7 @@
     widths = [part * eighth for part in RUNS] if vectors % 8 == 0 else [vectors]
     starts = [sum(widths[:i]) for i in range(len(widths))]
     last = len(widths) - 1
+    groups = [[0], list(range(1, last + 1))] if last else [[0]]
     live = call_mask(meta, wavefunction, starts, widths)
     extras = ()
     if ways == 2 and SPARE:
@@ -421,31 +422,36 @@
         return total, ticks[0]
 
     send(0)
-    *totals, tick = terms([None], [[around(wavefunction[0])]], left_env, right_env, extras, mask=True, split=widths)
+    split = [sum(widths[index] for index in group) for group in groups]
+    *totals, tick = terms([None], [[around(wavefunction[0])]], left_env, right_env, extras, mask=True, split=split)
     if last:
         send(1, tick)
     if ways_across:
         receive(0, tick)
-        for index in range(last + 1):
-            if index == last and index > 1:
-                share_far(index, tick)
-                totals[index], tick = add([index], totals[index], (0, 1), [tick])
-                continue
-            total, tick = add([index], totals[index], (0,), [tick])
-            share_far(index, tick)
-            if index + 1 <= last:
-                receive(index + 1, tick)
-            if index + 2 <= last:
-                send(index + 2, tick)
-            totals[index], tick = add([index], total, (1,), [tick])
-
-    blocks = []
-    for index in range(last + 1):
-        sums, *gifts = totals[index] if ways_across else (totals[index][:, :share],)
+        total, tick = add([0], totals[0], (0,), [tick])
+        share_far(0, tick)
+        if last:
+            receive(1, tick)
+        if last > 1:
+            send(2, tick)
+        totals[0], tick = add([0], total, (1,), [tick])
+        if last:
+            if last > 1:
+                receive(2, tick)
+            share_far(1, tick)
+            total, tick = add(groups[1], totals[1], (0,), [tick])
+            if last > 1:
+                share_far(2, tick)
+            totals[1], tick = add(groups[1], total, (1,), [tick])
+
+    product = jnp.zeros_like(wavefunction[0])
+    for number, group in enumerate(groups):
+        sums, *gifts = totals[number] if ways_across else (totals[number][:, :share],)
         for turn, given in enumerate(gifts, 1):
             sums += permute(given, "mpo", [(i, (i + turn) % ways) for i in range(ways)]).astype(jnp.float32)
-        blocks.append(jnp.where(keep_mask, sums, jnp.zeros_like(sums)).astype(jnp.bfloat16))
-    return jnp.concatenate(blocks)[None]
+        block = jnp.where(keep_mask, sums, jnp.zeros_like(sums)).astype(jnp.bfloat16)
+        product = lax.dynamic_update_slice(product, block, (starts[group[0]], 0, 0))
+    return product[None]
 
 
 def solution(mesh):

time: 94.2 us -> 93.5 us (level); the launches traced: 94.5 us -> 92.4 us
  waiting for transfers between devices: 31 us -> 26.1 us
  starting transfers between devices: 14.5 us -> 18.9 us
  Pallas kernels: 39.2 us -> 37.6 us
    ppermute x11 -> x15, waiting for transfers between devices: 31 us -> 26.1 us  [permute(): lax.ppermute(array, axis, sorted(pairs))]
    ppermute x11 -> x15, starting transfers between devices: 14.5 us -> 18.9 us  [permute(): lax.ppermute(array, axis, sorted(pairs))]
    pallas_call x5, Pallas kernels: 38.4 us -> 36.8 us  [call_terms(): pl.pallas_call(functools.partial(sum_terms, kinds, ways, slots, len(sourc...]
    unnamed x18 -> x16, local copies, waits for them, and re-layouts: 5.68 us -> 5.68 us
  transfers between devices with their start and end apart: 11 -> 15, of which waited for: 7 -> 6; matrix products, arithmetic and copies ran while one was open for 0% -> 0% of each run, Pallas kernels for 41% -> 41%
where the time goes in v4:
time: 93.5 us; the launch traced here: 92.4 us
  Pallas kernels  37.6 us (40%)
  waiting for transfers between devices  26.1 us (28%)
  starting transfers between devices  18.9 us (20%)
  local copies, waits for them, and re-layouts  5.77 us (6%)
  other arithmetic  2.61 us (3%)
  between operations  1.45 us (2%)
    pallas_call x5, Pallas kernels, call_terms(): pl.pallas_call(functools.partial(sum_terms, kinds, ways, slots, len(sourc...  36.8 us
    ppermute x15, waiting for transfers between devices, permute(): lax.ppermute(array, axis, sorted(pairs))  26.1 us
    ppermute x15, starting transfers between devices, permute(): lax.ppermute(array, axis, sorted(pairs))  18.9 us
    unnamed x16, local copies, waits for them, and re-layouts  5.68 us
  transfers between devices with their start and end apart: 15, of which 6 were waited for; matrix products, arithmetic and copies ran while one was open for 0% of the time, Pallas kernels for 41%

profile of v4, /device:TPU:25, one launch (start us, length us, event | category | flops | bytes accessed | tf_op | source)
XLA Modules:
  0.0 92.4 jit_solution(1015848671032663056)
XLA Ops:
  0.0 0.7 collective-permute-start.1
  2.1 1.2 %copy-done.1 = bf16[1,8,256,256]{3,2,1,0:T(8,128)(2,1)S(1)} copy-done((bf16[1,8,256,256]{3,2,1,0:T(8,128)(2,1)S(1)}, bf16[1,8,256,256]{3,2,1,0:T(8,128)(2,1)}, u32[]{:S(2)}) %copy-start.1) | copy-done | bytes 1048600
  3.3 0.7 shard_map.64
  4.0 1.0 %collective-permute-start = (bf16[3,256,256]{2,1,0:T(8,128)(2,1)S(1)}, bf16[3,256,256]{2,1,0:T(8,128)(2,1)S(1)}, u32[]{:S(2)}, u32[]{:S(2)}) collective-permute-start(bf16[3,256,256]{2,1,0:T(8,128)(2,1)S(1)} %get-tuple-element.36), channel_id=1, source_target_pairs={{0,18},{2,16},{4,22},{6,20},{8,26},{10,24},{12,30},{14,28},{16,2},... | collective-permute-start | bytes 1179656 | tf_op jit(solution)/shard_map/ppermute | solution.py:320
  5.1 13.8 %shard_map.65 = (f32[3,512,256]{2,1,0:T(8,128)}, f32[5,512,256]{2,1,0:T(8,128)}, s32[8,128]{1,0:T(8,128)}) custom-call(s32[20]{0:T(128)} %shift_ref.9, s32[10]{0:T(128)} %copy-done.5, bf16[8,256,256]{2,1,0:T(8,128)(2,1)} %bitcast.15, bf16[8,256,256]{2,1,0:T(8,128)(2,1)} %collective-permute-done.1.refs_1_, bf16[1,20,512,512]{3,2,1,0:T(8,128)(2,1)} %refs_4_.3, ...), custom_call_target="tpu_custom_call" | custom-call | flops 1000000 | bytes 1000 | tf_op jit(solution)/shard_map/pallas_call | solution.py:278
  18.9 6.4 %collective-permute-done.refs_0_ = bf16[3,256,256]{2,1,0:T(8,128)(2,1)S(1)} collective-permute-done((bf16[3,256,256]{2,1,0:T(8,128)(2,1)S(1)}, bf16[3,256,256]{2,1,0:T(8,128)(2,1)S(1)}, u32[]{:S(2)}, u32[]{:S(2)}) %collective-permute-start) | collective-permute-done | bytes 393248 | tf_op jit(solution)/shard_map/ppermute | solution.py:320
  25.7 3.1 %collective-permute-start.2 = (bf16[3,256,256]{2,1,0:T(8,128)(2,1)S(1)}, bf16[3,256,256]{2,1,0:T(8,128)(2,1)S(1)}, u32[]{:S(2)}, u32[]{:S(2)}) collective-permute-start(bf16[3,256,256]{2,1,0:T(8,128)(2,1)S(1)} %collective-permute-done.refs_0_), channel_id=1, source_target_pairs={{0,4},{4,8},{6,2},{8,12},{10,6},{14,10},{16,20},{20,24},{22,18},{2... | collective-permute-start | bytes 1179656 | tf_op jit(solution)/shard_map/ppermute | solution.py:320
  28.9 1.0 %collective-permute-start.6 = (bf16[3,256,256]{2,1,0:T(8,128)(2,1)S(1)}, bf16[3,256,256]{2,1,0:T(8,128)(2,1)S(1)}, u32[]{:S(2)}, u32[]{:S(2)}) collective-permute-start(bf16[3,256,256]{2,1,0:T(8,128)(2,1)S(1)} %get-tuple-element.48), channel_id=1, source_target_pairs={{0,18},{2,16},{4,22},{6,20},{8,26},{10,24},{12,30},{14,28},{16,2},... | collective-permute-start | bytes 1179656 | tf_op jit(solution)/shard_map/ppermute | solution.py:320
  29.9 1.7 %copy-done = bf16[1,20,256,256]{3,2,1,0:T(8,128)(2,1)S(1)} copy-done((bf16[1,20,256,256]{3,2,1,0:T(8,128)(2,1)S(1)}, bf16[1,20,256,256]{3,2,1,0:T(8,128)(2,1)}, u32[]{:S(2)}) %copy-start) | copy-done | bytes 2621464
  31.7 1.4 %copy-done.3 = f32[3,512,256]{2,1,0:T(8,128)S(1)} copy-done((f32[3,512,256]{2,1,0:T(8,128)S(1)}, f32[3,512,256]{2,1,0:T(8,128)}, u32[]{:S(2)}) %copy-start.3) | copy-done | bytes 1572888
  33.1 0.7 copy-done.4
  33.8 0.6 copy-done.6
  34.4 5.2 %shard_map.66 = (f32[3,512,256]{2,1,0:T(8,128)S(1)}, s32[8,128]{1,0:T(8,128)S(1)}) custom-call(s32[20]{0:T(128)S(1)} %copy-done.7, s32[10]{0:T(128)S(1)} %copy-done.6, bf16[3,256,256]{2,1,0:T(8,128)(2,1)S(1)} %collective-permute-done.refs_0_, bf16[3,256,256]{2,1,0:T(8,128)(2,1)S(1)} %collective-permute-done.3.refs_1_, bf16[1,20,512,512]{3,2,1,0:T(8,128)(2,1)} %refs_4_.3, ...), custom_call_target="tpu_custom_call" | custom-call | flops 1000000 | bytes 1000 | tf_op jit(solution)/shard_map/pallas_call | solution.py:278
  39.6 4.9 %collective-permute-done.2.refs_0_ = bf16[3,256,256]{2,1,0:T(8,128)(2,1)S(1)} collective-permute-done((bf16[3,256,256]{2,1,0:T(8,128)(2,1)S(1)}, bf16[3,256,256]{2,1,0:T(8,128)(2,1)S(1)}, u32[]{:S(2)}, u32[]{:S(2)}) %collective-permute-start.2) | collective-permute-done | bytes 393248 | tf_op jit(solution)/shard_map/ppermute | solution.py:320
  44.5 0.9 collective-permute-start.4
  45.4 1.8 %collective-permute-start.9 = (bf16[2,256,256]{2,1,0:T(8,128)(2,1)S(1)}, bf16[2,256,256]{2,1,0:T(8,128)(2,1)S(1)}, u32[]{:S(2)}, u32[]{:S(2)}) collective-permute-start(bf16[2,256,256]{2,1,0:T(8,128)(2,1)S(1)} %get-tuple-element.53), channel_id=1, source_target_pairs={{0,18},{2,16},{4,22},{6,20},{8,26},{10,24},{12,30},{14,28},{16,2},... | collective-permute-start | bytes 786440 | tf_op jit(solution)/shard_map/ppermute | solution.py:320
  47.2 5.7 %collective-permute-done.6.refs_0_ = bf16[3,256,256]{2,1,0:T(8,128)(2,1)S(1)} collective-permute-done((bf16[3,256,256]{2,1,0:T(8,128)(2,1)S(1)}, bf16[3,256,256]{2,1,0:T(8,128)(2,1)S(1)}, u32[]{:S(2)}, u32[]{:S(2)}) %collective-permute-start.6) | collective-permute-done | bytes 393248 | tf_op jit(solution)/shard_map/ppermute | solution.py:320
  52.9 1.9 %collective-permute-start.7 = (bf16[3,256,256]{2,1,0:T(8,128)(2,1)S(1)}, bf16[3,256,256]{2,1,0:T(8,128)(2,1)S(1)}, u32[]{:S(2)}, u32[]{:S(2)}) collective-permute-start(bf16[3,256,256]{2,1,0:T(8,128)(2,1)S(1)} %collective-permute-done.6.refs_0_), channel_id=1, source_target_pairs={{0,4},{4,8},{6,2},{8,12},{10,6},{14,10},{16,20},{20,24},{22,18},{2... | collective-permute-start | bytes 1179656 | tf_op jit(solution)/shard_map/ppermute | solution.py:320
  54.8 0.6 collective-permute-start.11
  55.4 4.6 %shard_map.67 = (f32[3,256,256]{2,1,0:T(8,128)S(1)}, bf16[3,256,256]{2,1,0:T(8,128)(2,1)S(1)}, s32[8,128]{1,0:T(8,128)S(1)}) custom-call(s32[20]{0:T(128)S(1)} %copy-done.7, s32[10]{0:T(128)S(1)} %copy-done.6, bf16[3,256,256]{2,1,0:T(8,128)(2,1)S(1)} %collective-permute-done.2.refs_0_, bf16[3,256,256]{2,1,0:T(8,128)(2,1)S(1)} %collective-permute-done.4.refs_1_, ...), custom_call_target="tpu_custom_call" | custom-call | flops 1000000 | bytes 1000 | tf_op jit(solution)/shard_map/pallas_call | solution.py:278
  60.0 1.5 %collective-permute-start.12 = (bf16[2,256,256]{2,1,0:T(8,128)(2,1)S(1)}, bf16[2,256,256]{2,1,0:T(8,128)(2,1)S(1)}, u32[]{:S(2)}, u32[]{:S(2)}) collective-permute-start(bf16[2,256,256]{2,1,0:T(8,128)(2,1)S(1)} %collective-permute-done.9.refs_2_), channel_id=1, source_target_pairs={{0,1},{1,0},{2,3},{3,2},{4,5},{5,4},{6,7},{7,6},{8,9},{9,8},{10,11... | collective-permute-start | bytes 786440 | tf_op jit(solution)/shard_map/ppermute | solution.py:320
  61.5 1.9 %collective-permute-start.10 = (bf16[2,256,256]{2,1,0:T(8,128)(2,1)S(1)}, bf16[2,256,256]{2,1,0:T(8,128)(2,1)S(1)}, u32[]{:S(2)}, u32[]{:S(2)}) collective-permute-start(bf16[2,256,256]{2,1,0:T(8,128)(2,1)S(1)} %collective-permute-done.9.refs_2_), channel_id=1, source_target_pairs={{0,4},{4,8},{6,2},{8,12},{10,6},{14,10},{16,20},{20,24},{22,18},{2... | collective-permute-start | bytes 786440 | tf_op jit(solution)/shard_map/ppermute | solution.py:320
  63.4 6.5 %collective-permute-done.7.refs_0_ = bf16[3,256,256]{2,1,0:T(8,128)(2,1)S(1)} collective-permute-done((bf16[3,256,256]{2,1,0:T(8,128)(2,1)S(1)}, bf16[3,256,256]{2,1,0:T(8,128)(2,1)S(1)}, u32[]{:S(2)}, u32[]{:S(2)}) %collective-permute-start.7) | collective-permute-done | bytes 393248 | tf_op jit(solution)/shard_map/ppermute | solution.py:320
  69.9 0.6 collective-permute-start.8
  70.5 7.1 %shard_map.68 = (f32[5,512,256]{2,1,0:T(8,128)S(1)}, s32[8,128]{1,0:T(8,128)S(1)}) custom-call(s32[20]{0:T(128)S(1)} %copy-done.7, s32[10]{0:T(128)S(1)} %copy-done.6, bf16[3,256,256]{2,1,0:T(8,128)(2,1)S(1)} %collective-permute-done.6.refs_0_, bf16[3,256,256]{2,1,0:T(8,128)(2,1)S(1)} %collective-permute-done.11.refs_1_, ...), custom_call_target="tpu_custom_call" | custom-call | flops 1000000 | bytes 1000 | tf_op jit(solution)/shard_map/pallas_call | solution.py:278
  77.7 0.5 collective-permute-start.5
  78.2 1.0 %collective-permute-done.13.refs_3_ = bf16[2,256,256]{2,1,0:T(8,128)(2,1)S(1)} collective-permute-done((bf16[2,256,256]{2,1,0:T(8,128)(2,1)S(1)}, bf16[2,256,256]{2,1,0:T(8,128)(2,1)S(1)}, u32[]{:S(2)}, u32[]{:S(2)}) %collective-permute-start.13) | collective-permute-done | bytes 262176 | tf_op jit(solution)/shard_map/ppermute | solution.py:320
  79.2 6.2 %shard_map.69 = (f32[5,256,256]{2,1,0:T(8,128)S(1)}, bf16[5,256,256]{2,1,0:T(8,128)(2,1)S(1)}, s32[8,128]{1,0:T(8,128)}) custom-call(s32[20]{0:T(128)S(1)} %copy-done.7, s32[10]{0:T(128)S(1)} %copy-done.6, bf16[3,256,256]{2,1,0:T(8,128)(2,1)S(1)} %collective-permute-done.7.refs_0_, bf16[3,256,256]{2,1,0:T(8,128)(2,1)S(1)} %collective-permute-done.8.refs_1_, ...), custom_call_target="tpu_custom_call" | custom-call | flops 1000000 | bytes 1000 | tf_op jit(solution)/shard_map/pallas_call | solution.py:278
  85.4 2.8 %collective-permute-start.14 = (bf16[5,256,256]{2,1,0:T(8,128)(2,1)S(1)}, bf16[5,256,256]{2,1,0:T(8,128)(2,1)}, u32[]{:S(2)}, u32[]{:S(2)}) collective-permute-start(bf16[5,256,256]{2,1,0:T(8,128)(2,1)S(1)} %get-tuple-element.66), channel_id=1, source_target_pairs={{0,1},{1,0},{2,3},{3,2},{4,5},{5,4},{6,7},{7,6},{8,9},{9,8},{10,11... | collective-permute-start | bytes 1966088 | tf_op jit(solution)/shard_map/ppermute | solution.py:320
  88.5 1.6 %collective-permute-done.14 = bf16[5,256,256]{2,1,0:T(8,128)(2,1)} collective-permute-done((bf16[5,256,256]{2,1,0:T(8,128)(2,1)S(1)}, bf16[5,256,256]{2,1,0:T(8,128)(2,1)}, u32[]{:S(2)}, u32[]{:S(2)}) %collective-permute-start.14) | collective-permute-done | bytes 655392 | tf_op jit(solution)/shard_map/ppermute | solution.py:320
  90.1 1.3 %select_convert_fusion = bf16[5,256,256]{2,1,0:T(8,128)(2,1)S(1)} fusion(f32[5,256,256]{2,1,0:T(8,128)S(1)} %get-tuple-element.65, bf16[5,256,256]{2,1,0:T(8,128)(2,1)} %collective-permute-done.14, pred[256,256]{1,0:T(8,128)(4,1)S(1)} %broadcast_and_fusion), kind=kLoop, calls=%fused_computation | loop fusion | flops 1310720 | bytes 2686976 | tf_op jit(solution)/shard_map/convert_element_type | solution.py:452
  91.3 1.1 %maximum_bitcast_fusion = bf16[1,8,256,256]{3,2,1,0:T(8,128)(2,1)} fusion(bf16[5,256,256]{2,1,0:T(8,128)(2,1)S(1)} %select_convert_fusion, bf16[3,256,256]{2,1,0:T(8,128)(2,1)S(1)} %select_convert_fusion.1), kind=kLoop, calls=%fused_computation.1 | loop fusion | flops 524288 | bytes 2097152 | tf_op jit(solution)/shard_map/broadcast_in_dim | solution.py:454
  (26 shorter events, 0.9 us)
Async XLA Ops:
  0.0 5.1 %collective-permute-start.1 = (bf16[8,256,256]{2,1,0:T(8,128)(2,1)}, bf16[8,256,256]{2,1,0:T(8,128)(2,1)}, u32[]{:S(2)}, u32[]{:S(2)}) collective-permute-start(bf16[8,256,256]{2,1,0:T(8,128)(2,1)} %bitcast.14), channel_id=1, source_target_pairs={{0,1},{1,0},{2,3},{3,2},{4,5},{5,4},{6,7},{7,6},{8,9},{9,8},{10,11... | collective-permute-start | bytes 3145736 | tf_op jit(solution)/shard_map/ppermute | solution.py:320
  2.1 1.2 %copy-start.1 = (bf16[1,8,256,256]{3,2,1,0:T(8,128)(2,1)S(1)}, bf16[1,8,256,256]{3,2,1,0:T(8,128)(2,1)}, u32[]{:S(2)}) copy-start(bf16[1,8,256,256]{3,2,1,0:T(8,128)(2,1)} %source_ref.1) | copy-start | bytes 3145732
  3.3 1.8 %copy-start.5 = (s32[10]{0:T(128)}, s32[10]{0:T(128)S(1)}, u32[]{:S(2)}) copy-start(s32[10]{0:T(128)S(1)} %stack.47.meta_ref) | copy-start | bytes 124
  4.0 25.9 %copy-start.7 = (s32[20]{0:T(128)S(1)}, s32[20]{0:T(128)}, u32[]{:S(2)}) copy-start(s32[20]{0:T(128)} %shift_ref.9) | copy-start | bytes 244
  4.0 21.3 %collective-permute-start = (bf16[3,256,256]{2,1,0:T(8,128)(2,1)S(1)}, bf16[3,256,256]{2,1,0:T(8,128)(2,1)S(1)}, u32[]{:S(2)}, u32[]{:S(2)}) collective-permute-start(bf16[3,256,256]{2,1,0:T(8,128)(2,1)S(1)} %get-tuple-element.36), channel_id=1, source_target_pairs={{0,18},{2,16},{4,22},{6,20},{8,26},{10,24},{12,30},{14,28},{16,2},... | collective-permute-start | bytes 1179656 | tf_op jit(solution)/shard_map/ppermute | solution.py:320
  25.3 4.6 %collective-permute-start.3 = (bf16[3,256,256]{2,1,0:T(8,128)(2,1)S(1)}, bf16[3,256,256]{2,1,0:T(8,128)(2,1)S(1)}, u32[]{:S(2)}, u32[]{:S(2)}) collective-permute-start(bf16[3,256,256]{2,1,0:T(8,128)(2,1)S(1)} %collective-permute-done.refs_0_), channel_id=1, source_target_pairs={{0,1},{1,0},{2,3},{3,2},{4,5},{5,4},{6,7},{7,6},{8,9},{9,8},{10,11... | collective-permute-start | bytes 1179656 | tf_op jit(solution)/shard_map/ppermute | solution.py:320
  25.7 18.7 %collective-permute-start.2 = (bf16[3,256,256]{2,1,0:T(8,128)(2,1)S(1)}, bf16[3,256,256]{2,1,0:T(8,128)(2,1)S(1)}, u32[]{:S(2)}, u32[]{:S(2)}) collective-permute-start(bf16[3,256,256]{2,1,0:T(8,128)(2,1)S(1)} %collective-permute-done.refs_0_), channel_id=1, source_target_pairs={{0,4},{4,8},{6,2},{8,12},{10,6},{14,10},{16,20},{20,24},{22,18},{2... | collective-permute-start | bytes 1179656 | tf_op jit(solution)/shard_map/ppermute | solution.py:320
  28.9 24.0 %collective-permute-start.6 = (bf16[3,256,256]{2,1,0:T(8,128)(2,1)S(1)}, bf16[3,256,256]{2,1,0:T(8,128)(2,1)S(1)}, u32[]{:S(2)}, u32[]{:S(2)}) collective-permute-start(bf16[3,256,256]{2,1,0:T(8,128)(2,1)S(1)} %get-tuple-element.48), channel_id=1, source_target_pairs={{0,18},{2,16},{4,22},{6,20},{8,26},{10,24},{12,30},{14,28},{16,2},... | collective-permute-start | bytes 1179656 | tf_op jit(solution)/shard_map/ppermute | solution.py:320
  29.9 1.7 %copy-start = (bf16[1,20,256,256]{3,2,1,0:T(8,128)(2,1)S(1)}, bf16[1,20,256,256]{3,2,1,0:T(8,128)(2,1)}, u32[]{:S(2)}) copy-start(bf16[1,20,256,256]{3,2,1,0:T(8,128)(2,1)} %refs_5_.3) | copy-start | bytes 7864324
  31.7 1.4 %copy-start.3 = (f32[3,512,256]{2,1,0:T(8,128)S(1)}, f32[3,512,256]{2,1,0:T(8,128)}, u32[]{:S(2)}) copy-start(f32[3,512,256]{2,1,0:T(8,128)} %get-tuple-element.40.refs_6_) | copy-start | bytes 4718596
  33.1 0.7 copy-start.4
  33.8 0.6 copy-start.6
  44.5 10.9 %collective-permute-start.4 = (bf16[3,256,256]{2,1,0:T(8,128)(2,1)S(1)}, bf16[3,256,256]{2,1,0:T(8,128)(2,1)S(1)}, u32[]{:S(2)}, u32[]{:S(2)}) collective-permute-start(bf16[3,256,256]{2,1,0:T(8,128)(2,1)S(1)} %collective-permute-done.2.refs_0_), channel_id=1, source_target_pairs={{0,1},{1,0},{2,3},{3,2},{4,5},{5,4},{6,7},{7,6},{8,9},{9,8},{10,11... | collective-permute-start | bytes 1179656 | tf_op jit(solution)/shard_map/ppermute | solution.py:320
  45.4 14.6 %collective-permute-start.9 = (bf16[2,256,256]{2,1,0:T(8,128)(2,1)S(1)}, bf16[2,256,256]{2,1,0:T(8,128)(2,1)S(1)}, u32[]{:S(2)}, u32[]{:S(2)}) collective-permute-start(bf16[2,256,256]{2,1,0:T(8,128)(2,1)S(1)} %get-tuple-element.53), channel_id=1, source_target_pairs={{0,18},{2,16},{4,22},{6,20},{8,26},{10,24},{12,30},{14,28},{16,2},... | collective-permute-start | bytes 786440 | tf_op jit(solution)/shard_map/ppermute | solution.py:320
  52.9 17.1 %collective-permute-start.7 = (bf16[3,256,256]{2,1,0:T(8,128)(2,1)S(1)}, bf16[3,256,256]{2,1,0:T(8,128)(2,1)S(1)}, u32[]{:S(2)}, u32[]{:S(2)}) collective-permute-start(bf16[3,256,256]{2,1,0:T(8,128)(2,1)S(1)} %collective-permute-done.6.refs_0_), channel_id=1, source_target_pairs={{0,4},{4,8},{6,2},{8,12},{10,6},{14,10},{16,20},{20,24},{22,18},{2... | collective-permute-start | bytes 1179656 | tf_op jit(solution)/shard_map/ppermute | solution.py:320
  54.8 15.7 %collective-permute-start.11 = (bf16[3,256,256]{2,1,0:T(8,128)(2,1)S(1)}, bf16[3,256,256]{2,1,0:T(8,128)(2,1)S(1)}, u32[]{:S(2)}, u32[]{:S(2)}) collective-permute-start(bf16[3,256,256]{2,1,0:T(8,128)(2,1)S(1)} %collective-permute-done.6.refs_0_), channel_id=1, source_target_pairs={{0,1},{1,0},{2,3},{3,2},{4,5},{5,4},{6,7},{7,6},{8,9},{9,8},{10,11... | collective-permute-start | bytes 1179656 | tf_op jit(solution)/shard_map/ppermute | solution.py:320
  55.4 15.1 %copy-start.2 = (f32[5,512,256]{2,1,0:T(8,128)S(1)}, f32[5,512,256]{2,1,0:T(8,128)}, u32[]{:S(2)}) copy-start(f32[5,512,256]{2,1,0:T(8,128)} %get-tuple-element.59.refs_11_) | copy-start | bytes 7864324
  60.0 10.5 %collective-permute-start.12 = (bf16[2,256,256]{2,1,0:T(8,128)(2,1)S(1)}, bf16[2,256,256]{2,1,0:T(8,128)(2,1)S(1)}, u32[]{:S(2)}, u32[]{:S(2)}) collective-permute-start(bf16[2,256,256]{2,1,0:T(8,128)(2,1)S(1)} %collective-permute-done.9.refs_2_), channel_id=1, source_target_pairs={{0,1},{1,0},{2,3},{3,2},{4,5},{5,4},{6,7},{7,6},{8,9},{9,8},{10,11... | collective-permute-start | bytes 786440 | tf_op jit(solution)/shard_map/ppermute | solution.py:320
  61.5 16.1 %collective-permute-start.10 = (bf16[2,256,256]{2,1,0:T(8,128)(2,1)S(1)}, bf16[2,256,256]{2,1,0:T(8,128)(2,1)S(1)}, u32[]{:S(2)}, u32[]{:S(2)}) collective-permute-start(bf16[2,256,256]{2,1,0:T(8,128)(2,1)S(1)} %collective-permute-done.9.refs_2_), channel_id=1, source_target_pairs={{0,4},{4,8},{6,2},{8,12},{10,6},{14,10},{16,20},{20,24},{22,18},{2... | collective-permute-start | bytes 786440 | tf_op jit(solution)/shard_map/ppermute | solution.py:320
  69.9 8.3 %collective-permute-start.8 = (bf16[3,256,256]{2,1,0:T(8,128)(2,1)S(1)}, bf16[3,256,256]{2,1,0:T(8,128)(2,1)S(1)}, u32[]{:S(2)}, u32[]{:S(2)}) collective-permute-start(bf16[3,256,256]{2,1,0:T(8,128)(2,1)S(1)} %collective-permute-done.7.refs_0_), channel_id=1, source_target_pairs={{0,1},{1,0},{2,3},{3,2},{4,5},{5,4},{6,7},{7,6},{8,9},{9,8},{10,11... | collective-permute-start | bytes 1179656 | tf_op jit(solution)/shard_map/ppermute | solution.py:320
  77.6 1.6 %collective-permute-start.13 = (bf16[2,256,256]{2,1,0:T(8,128)(2,1)S(1)}, bf16[2,256,256]{2,1,0:T(8,128)(2,1)S(1)}, u32[]{:S(2)}, u32[]{:S(2)}) collective-permute-start(bf16[2,256,256]{2,1,0:T(8,128)(2,1)S(1)} %collective-permute-done.10.refs_2_), channel_id=1, source_target_pairs={{0,1},{1,0},{2,3},{3,2},{4,5},{5,4},{6,7},{7,6},{8,9},{9,8},{10,11... | collective-permute-start | bytes 786440 | tf_op jit(solution)/shard_map/ppermute | solution.py:320
  77.7 10.6 %collective-permute-start.5 = (bf16[3,256,256]{2,1,0:T(8,128)(2,1)S(1)}, bf16[3,256,256]{2,1,0:T(8,128)(2,1)S(1)}, u32[]{:S(2)}, u32[]{:S(2)}) collective-permute-start(bf16[3,256,256]{2,1,0:T(8,128)(2,1)S(1)} %get-tuple-element.46), channel_id=1, source_target_pairs={{0,1},{1,0},{2,3},{3,2},{4,5},{5,4},{6,7},{7,6},{8,9},{9,8},{10,11... | collective-permute-start | bytes 1179656 | tf_op jit(solution)/shard_map/ppermute | solution.py:320
  85.4 4.7 %collective-permute-start.14 = (bf16[5,256,256]{2,1,0:T(8,128)(2,1)S(1)}, bf16[5,256,256]{2,1,0:T(8,128)(2,1)}, u32[]{:S(2)}, u32[]{:S(2)}) collective-permute-start(bf16[5,256,256]{2,1,0:T(8,128)(2,1)S(1)} %get-tuple-element.66), channel_id=1, source_target_pairs={{0,1},{1,0},{2,3},{3,2},{4,5},{5,4},{6,7},{7,6},{8,9},{9,8},{10,11... | collective-permute-start | bytes 1966088 | tf_op jit(solution)/shard_map/ppermute | solution.py:320
